TPU v7x, 32 devices: a whole 2x2x4 slice. The times are simulated.
32 devices in a mesh: narrow: 4 (over x, core), wide: 8 (over z, y).
Axes of the slice: x: 2, y: 2, z: 4, core: 2. Of those that a mesh axis runs over, the one named last changes fastest.
Arguments:
- block_input: bfloat16 [32, 14, 14, 2048], P('wide', None, None, 'narrow'), may hold values from -8 to 8, as said below
- out_grad: bfloat16 [32, 14, 14, 2048], P('wide', None, None, 'narrow'), may hold values from -6 to 6
- conv_reduce: float32 [2, 2048, 512], P(None, 'wide', 'narrow'), may hold values from -2 to 2, as said below
- conv_spatial: float32 [2, 4608, 512], P(None, 'wide', 'narrow'), may hold values from -2 to 2, as said below
- conv_expand: float32 [2, 512, 2048], P(None, 'wide', 'narrow'), may hold values from -2 to 2, as said below
- first_reduce: float32 [2, 2048, 512], P(None, 'wide', 'narrow'), may hold values from -56 to 56
- first_spatial: float32 [2, 4608, 512], P(None, 'wide', 'narrow'), may hold values from -56 to 56
- first_expand: float32 [2, 512, 2048], P(None, 'wide', 'narrow'), may hold values from -56 to 56
- second_reduce: float32 [2, 2048, 512], P(None, 'wide', 'narrow'), may hold values from 6.272 to 25.088
- second_spatial: float32 [2, 4608, 512], P(None, 'wide', 'narrow'), may hold values from 6.272 to 25.088
- second_expand: float32 [2, 512, 2048], P(None, 'wide', 'narrow'), may hold values from 6.272 to 25.088
- norm_params: float32 [2, 2, 4, 768], P(None, None, 'narrow'), may hold values from -1 to 2, as said below
- norm_first: float32 [2, 2, 4, 768], P(None, None, 'narrow'), may hold values from -56 to 56
- norm_second: float32 [2, 2, 4, 768], P(None, None, 'narrow'), may hold values from 6.272 to 25.088
Outputs:
- block_output: float32 [32, 14, 14, 2048], P('wide', None, None, 'narrow')
- input_grad: float32 [32, 14, 14, 2048], P('wide', None, None, 'narrow')
- grad_reduce: float32 [2, 2048, 512], P(None, 'wide', 'narrow')
- grad_spatial: float32 [2, 4608, 512], P(None, 'wide', 'narrow')
- grad_expand: float32 [2, 512, 2048], P(None, 'wide', 'narrow')
- square_reduce: float32 [2, 2048, 512], P(None, 'wide', 'narrow')
- square_spatial: float32 [2, 4608, 512], P(None, 'wide', 'narrow')
- square_expand: float32 [2, 512, 2048], P(None, 'wide', 'narrow')
- new_reduce: float32 [2, 2048, 512], P(None, 'wide', 'narrow')
- new_spatial: float32 [2, 4608, 512], P(None, 'wide', 'narrow')
- new_expand: float32 [2, 512, 2048], P(None, 'wide', 'narrow')
- norm_grads: float32 [2, 2, 4, 768], P(None, None, 'narrow')
- norm_square: float32 [2, 2, 4, 768], P(None, None, 'narrow')
- norm_new: float32 [2, 2, 4, 768], P(None, None, 'narrow')
- layer_norms: float32 [2, 3, 2], replicated
Inputs may be any that keep to these rules, and one draw needn't show every extreme that they name: `block_input`: real-valued activations. `norm_params`: gains near one and shifts near zero. `conv_reduce`: real-valued weights. `conv_spatial`: real-valued weights. `conv_expand`: real-valued weights.
All inputs are finite; a program needn't handle non-finite values.
Results may differ from a plain program's by a relative error of at most 0.024.
Values may be sent and summed in bfloat16 or wider, within the bound.
No kernel may reach another device: no remote copies, remote signals or barrier semaphores. Data moves between devices by JAX's collectives and lax.ppermute only.
A program may use at most 192 MiB of HBM per device.

v0:
```python
import functools

import jax
import jax.numpy as jnp
import numpy as np
from jax import lax
from jax.experimental import pallas as pl
from jax.experimental.pallas import tpu as pltpu
from jax.sharding import Mesh
from jax.sharding import PartitionSpec as P

STEP = 10
BN_EPS = 1e-05
FIRST_DECAY = 0.9
SECOND_DECAY = 0.999
ADAM_EPSILON = 1e-06
WEIGHT_DECAY = 0.01
MATRIX_RATE = 0.5
NORM_RATE = 0.3

ALL = ("x", "core", "wide")
CROSS = ("x", "wide")
BF = jnp.bfloat16
F32 = jnp.float32

SIDE = 14
LINE = 16
IMG = SIDE * LINE
NIMG = 2
ROWS = NIMG * IMG
SPAN = ROWS + LINE * (NIMG - 1)
PIECES = 8


def dot(a, b):
    return lax.dot_general(a, b, (((1,), (0,)), ((), ())), preferred_element_type=F32)


def dot_nt(a, b):
    return lax.dot_general(a, b, (((1,), (1,)), ((), ())), preferred_element_type=F32)


def dot_tn(a, b):
    return lax.dot_general(a, b, (((0,), (0,)), ((), ())), preferred_element_type=F32)


def lanes(parts):
    return jnp.concatenate(parts, axis=1)


def rows(parts):
    return jnp.concatenate(parts, axis=0)


def sigmoid(v):
    return 0.5 * jnp.tanh(0.5 * v) + 0.5


def silu(v):
    return v * sigmoid(v)


def silu_slope(v):
    s = sigmoid(v)
    return s * (1.0 + v * (1.0 - s))


def inside(shape):
    return (lax.broadcasted_iota(jnp.int32, shape, 0) & (LINE - 1)) < SIDE


def keep_inside(v):
    return jnp.where(inside(v.shape), v, 0.0)


def pack_rows(total, other):
    n = total.shape[1] // 128
    return rows([v[:, i * 128 : (i + 1) * 128] for v in (total, other) for i in range(n)])


def unpack_rows(block):
    n = block.shape[0] // 2
    return tuple(lanes([block[k * n + i : k * n + i + 1] for i in range(n)]) for k in range(2))


def column_sums(a, b):
    return pack_rows(jnp.sum(a, 0, keepdims=True), jnp.sum(b, 0, keepdims=True))


def mean_inverse(block, population):
    total, square = unpack_rows(block)
    mean = total / population
    return mean, lax.rsqrt(square / population - mean * mean + BN_EPS)


class Late:
    def __init__(self, buf, copy):
        self.buf = buf
        self.copy = copy
        self.shape = buf.shape
        self.waited = False
        copy.start()

    def wait(self):
        if not self.waited:
            self.copy.wait()
            self.waited = True

    def __getitem__(self, at):
        self.wait()
        return self.buf[at]


class Pair:
    def __init__(self, near, far):
        self.near = near
        self.far = far
        self.shape = near.shape

    def __getitem__(self, at):
        piece, rest = (at[0], at[1:]) if isinstance(at, tuple) else (at, ())
        inner = (piece & (PIECES - 1),) + rest
        return jnp.where(piece < PIECES, self.near[inner], self.far[inner])


def call(kernel, outs, *args, scratch=(), name=None, smem=(), limit=16, weight=None):
    vmem = pl.BlockSpec(memory_space=pltpu.VMEM)
    in_specs = [pl.BlockSpec(memory_space=pltpu.SMEM) if i in smem else vmem for i in range(len(args))]
    count = len(args)
    ins = list(args)
    scratch = list(scratch)
    cut = False
    if weight is not None:
        parts, (lo, hi) = weight
        ins += parts
        cut = parts[0].shape[1] != hi - lo
        in_specs += [pl.BlockSpec(memory_space=pl.ANY) if cut else vmem] * len(parts)
        if cut:
            scratch += [pltpu.VMEM((2 * PIECES, hi - lo, parts[0].shape[2]), BF), pltpu.SemaphoreType.DMA]
    total = len(ins)

    def whole(*refs):
        operands, results = refs[:count], refs[total:]
        if weight is None:
            return kernel(*operands, *results)
        held = refs[count:total]
        if not cut:
            return kernel(*operands, Pair(*held) if len(held) == 2 else held[0], *results)
        buf, sem = results[-2:]
        late = Late(buf, pltpu.make_async_copy(held[0].at[:, lo:hi], buf, sem))
        kernel(*operands, late, *results[:-2])
        late.wait()

    return pl.pallas_call(
        whole,
        out_shape=[jax.ShapeDtypeStruct(shape, dtype) for shape, dtype in outs],
        in_specs=in_specs,
        out_specs=[vmem] * len(outs),
        scratch_shapes=scratch,
        compiler_params=pltpu.CompilerParams(vmem_limit_bytes=limit * 1024 * 1024),
        name=name,
    )(*ins)


def place(ids, half, piece):
    return ids[4 + PIECES * half + piece]


def origin(ids, at):
    return ids[4 + 2 * PIECES + at]


def piece_of(ids, w, half, piece):
    return w[place(ids, half, piece)]


def expand_weights(ids, w, half):
    def piece(at):
        if w.shape[2] == 512:
            return w[at]
        depth = w.shape[1] // 4
        return lanes([w[at, i * depth : (i + 1) * depth] for i in range(4)])

    return rows([piece(place(ids, half, p)) for p in range(PIECES)])


def deal(ids, held, near, far):
    for start, dst in ((PIECES, far), (0, near)):
        for at in range(PIECES):
            dst[at] = held[origin(ids, start + at)]


def enter_kernel(ids, image_ref, grad_ref, keep_x, send_x, keep_g, send_g):
    x = ids[0]
    for src, keep, send in ((image_ref, keep_x, send_x), (grad_ref, keep_g, send_g)):
        for dst, owner in ((keep, x), (send, 1 - x)):
            for i in range(NIMG):
                img = src[owner * NIMG + i]
                pad = jnp.zeros((SIDE, LINE - SIDE, img.shape[2]), img.dtype)
                full = jnp.concatenate([img, pad], axis=1)
                dst[i * IMG : (i + 1) * IMG] = full.reshape(IMG, img.shape[2])


def join_kernel(ids, keep, recv, out):
    first = ids[0] == 0
    a = keep[...]
    b = recv[...]
    n = a.shape[1]
    out[:, :n] = jnp.where(first, a, b)
    out[:, n:] = jnp.where(first, b, a)


def params_kernel(ids, near_ref, far_ref, own_ref, oth_ref):
    first = ids[0] == 0
    for n, dst in ((0, own_ref), (1, oth_ref)):
        for lo, hi in ((0, 128), (128, 256), (256, 768)):
            a = near_ref[n, :, lo:hi]
            c = far_ref[n, :, lo:hi]
            dst[:, 2 * lo : lo + hi] = jnp.where(first, a, c)
            dst[:, lo + hi : 2 * hi] = jnp.where(first, c, a)


def centred(z, total, pixels):
    return keep_inside(z - total / pixels).astype(BF)


def reduce_kernel(ids, xo, xt, w, pre_out, centred_out, stat_out):
    core = ids[1]
    parts = []
    for c in (core, 1 - core):
        for k in range(2):
            for j in range(2):
                p = 2 * (2 * k + c) + j
                parts.append(lanes([piece_of(ids, w, 0, p), piece_of(ids, w, 1, p)]))
    pre = dot(lanes([xo[...], xt[...]]), rows(parts))
    total = jnp.sum(pre, 0, keepdims=True)
    stats = pack_rows(total, jnp.sum(pre * pre, 0, keepdims=True))
    pre_out[...] = pre
    centred_out[...] = centred(pre, total, NIMG * SIDE * SIDE)
    stat_out[...] = jnp.broadcast_to(stats[None], stat_out.shape)


def both_halves(ids, stat, pre, other, own_prm, oth_prm, lo, population, moments_out):
    x, core, wide = ids[0], ids[1], ids[2]
    own = stat[:, pl.ds(core, 1)]
    oth = stat[:, pl.ds(1 - core, 1)]
    own_sum = jnp.sum(own, axis=(0, 1, 2))
    oth_sum = jnp.sum(oth, axis=(0, 1, 2))
    local = stat[pl.ds(x, 1), pl.ds(1 - core, 1), pl.ds(wide, 1)].reshape(4, 128)
    mean, inverse = mean_inverse(own_sum, population)
    moments_out[...] = rows([mean, inverse, jnp.zeros((6, mean.shape[1]), F32)])
    hid_own = silu(own_prm[0:1, lo : lo + 256] * (pre[...] - mean) * inverse + own_prm[1:2, lo : lo + 256])
    mean_t, inverse_t = mean_inverse(oth_sum, population)
    local_mean = unpack_rows(local)[0] / (NIMG * SIDE * SIDE)
    hid_oth = silu(
        oth_prm[0:1, lo : lo + 256] * (other[...].astype(F32) + (local_mean - mean_t)) * inverse_t
        + oth_prm[1:2, lo : lo + 256]
    )
    hid_own = keep_inside(hid_own)
    hid_oth = keep_inside(hid_oth)
    first = core == 0
    parts = []
    for k in range(2):
        a = hid_own[:, k * 128 : (k + 1) * 128]
        b = hid_oth[:, k * 128 : (k + 1) * 128]
        parts += [jnp.where(first, a, b), jnp.where(first, b, a)]
    return lanes(parts)


def fill_shifts(dst, v, sign):
    for d in range(3):
        shifted = v if d == 1 else pltpu.roll(v, (sign * (d - 1)) % v.shape[0], 0)
        shifted = shifted.astype(BF)
        dst[d, 0:LINE] = jnp.zeros((LINE, v.shape[1]), BF)
        for i in range(NIMG):
            at = LINE + i * (IMG + LINE)
            dst[d, at : at + IMG] = shifted[i * IMG : (i + 1) * IMG]
            dst[d, at + IMG : at + IMG + LINE] = jnp.zeros((LINE, v.shape[1]), BF)


def squeeze(v):
    return rows([v[i * (IMG + LINE) : i * (IMG + LINE) + IMG] for i in range(NIMG)])


def tap_segments(tap, depth):
    lo, hi = tap * 512, (tap + 1) * 512
    found = []
    while lo < hi:
        piece = lo // depth
        end = min(hi, (piece + 1) * depth)
        found.append((piece, lo - piece * depth, end - piece * depth))
        lo = end
    return found


def tap_weights(ids, w, tap):
    return lanes(
        [
            rows([w[place(ids, h, p), a:b] for p, a, b in tap_segments(tap, w.shape[1])])
            for h in range(2)
        ]
    )


def spatial_kernel(
    population, ids, stat, pre, other, own_prm, oth_prm, w, hid_out, moments_out, pre_out, centred_out, stat_out, shifts
):
    hid = both_halves(ids, stat, pre, other, own_prm, oth_prm, 0, population, moments_out)
    fill_shifts(shifts, hid, -1)
    hid_out[...] = shifts[1, LINE : LINE + SPAN]
    acc = None
    for tap in range(9):
        at = (tap // 3) * LINE
        part = dot(shifts[tap % 3, at : at + SPAN], tap_weights(ids, w, tap))
        acc = part if acc is None else acc + part
    pre2 = keep_inside(squeeze(acc))
    total = jnp.sum(pre2, 0, keepdims=True)
    stats = pack_rows(total, jnp.sum(pre2 * pre2, 0, keepdims=True))
    pre_out[...] = pre2
    centred_out[...] = centred(pre2, total, NIMG * SIDE * SIDE)
    stat_out[...] = jnp.broadcast_to(stats[None], stat_out.shape)


def expand_kernel(population, ids, stat, pre, other, own_prm, oth_prm, w, hid_out, moments_out, pre_out, stat_out):
    hid = both_halves(ids, stat, pre, other, own_prm, oth_prm, 256, population, moments_out).astype(BF)
    hid_out[...] = hid
    total = []
    square = []
    for h in range(2):
        pre3 = dot(hid, expand_weights(ids, w, h))
        pre_out[:, h * 512 : (h + 1) * 512] = pre3
        total.append(jnp.sum(pre3, 0, keepdims=True))
        square.append(jnp.sum(pre3 * pre3, 0, keepdims=True))
    stats = pack_rows(lanes(total), lanes(square))
    stat_out[...] = jnp.broadcast_to(stats[None], stat_out.shape)


def close_kernel(population, stat, pre, stream, own_prm, moments_out, out, low_out):
    mean, inverse = mean_inverse(jnp.sum(stat[...], 0), population)
    moments_out[...] = rows([mean, inverse, jnp.zeros((6, mean.shape[1]), F32)])
    v = own_prm[0:1, 512:] * (pre[...] - mean) * inverse + own_prm[1:2, 512:] + stream[...].astype(F32)
    result = keep_inside(silu(v))
    out[...] = result
    low_out[...] = result.astype(BF)


def last_kernel(population, ids, stat, pre, stream, own_prm, keep_g, recv_g, moments_out, out, outside_out, stat_out):
    mean, inverse = mean_inverse(jnp.sum(stat[...], 0), population)
    moments_out[...] = rows([mean, inverse, jnp.zeros((6, mean.shape[1]), F32)])
    normed = (pre[...] - mean) * inverse
    v = own_prm[0:1, 512:] * normed + own_prm[1:2, 512:] + stream[...].astype(F32)
    s = sigmoid(v)
    out[...] = v * s
    first = ids[0] == 0
    a = keep_g[...]
    b = recv_g[...]
    grad = lanes([jnp.where(first, a, b), jnp.where(first, b, a)]).astype(F32)
    outside = keep_inside(grad * (s * (1.0 + v * (1.0 - s))))
    outside_out[...] = outside
    stat_out[...] = jnp.broadcast_to(column_sums(outside, outside * normed)[None], stat_out.shape)


def outer_back_kernel(moments, pre, stream, own_prm, outside_after, own_part, recv_part, outside_out, stat_out):
    mean = moments[0:1]
    inverse = moments[1:2]
    normed = (pre[...] - mean) * inverse
    v = own_prm[0:1, 512:] * normed + own_prm[1:2, 512:] + stream[...].astype(F32)
    upstream = outside_after[...] + own_part[...] + recv_part[...].astype(F32)
    outside = keep_inside(upstream * silu_slope(v))
    outside_out[...] = outside
    stat_out[...] = jnp.broadcast_to(column_sums(outside, outside * normed)[None], stat_out.shape)


def norm_back(sums, population, moments, pre, upstream, gain):
    shift_grad, gain_grad = unpack_rows(sums)
    mean = moments[0:1]
    inverse = moments[1:2]
    normed = (pre[...] - mean) * inverse
    lowered = gain * inverse * (upstream[...] - shift_grad / population - normed * (gain_grad / population))
    return keep_inside(lowered)


def split_cores(ids, parts, own_out, send_out):
    first = ids[1] == 0
    width = parts[0].shape[1]
    for k in range(2):
        a, b = parts[2 * k], parts[2 * k + 1]
        own_out[:, k * width : (k + 1) * width] = jnp.where(first, a, b)
        send_out[:, k * width : (k + 1) * width] = jnp.where(first, b, a).astype(BF)


def expand_back_kernel(population, ids, stat, moments, pre, outside, own_prm, w, low_out, own_out, send_out, sums_out):
    sums = jnp.sum(stat[...], 0)
    sums_out[...] = sums
    low = norm_back(sums, population, moments, pre, outside, own_prm[0:1, 512:]).astype(BF)
    low_out[...] = low
    acc = None
    for h in range(2):
        part = dot_nt(low[:, h * 512 : (h + 1) * 512], expand_weights(ids, w, h))
        acc = part if acc is None else acc + part
    split_cores(ids, [acc[:, n * 128 : (n + 1) * 128] for n in range(4)], own_out, send_out)


def expand_grad(ids, hid, low, held):
    grad = dot_tn(hid[...], low[...])
    lane_blocks = 512 // held.shape[2]
    depth = held.shape[1] // lane_blocks
    for h in range(2):
        for p in range(PIECES):
            piece = grad[p * depth : (p + 1) * depth, h * 512 : (h + 1) * 512].astype(BF)
            if lane_blocks == 1:
                held[h * PIECES + p] = piece
            else:
                for i in range(lane_blocks):
                    held[h * PIECES + p, i * depth : (i + 1) * depth] = piece[:, i * 128 : (i + 1) * 128]


def inner_back_kernel(lo, own_part, recv_part, moments, pre, own_prm, out, stat_out):
    normed = (pre[...] - moments[0:1]) * moments[1:2]
    v = own_prm[0:1, lo : lo + 256] * normed + own_prm[1:2, lo : lo + 256]
    upstream = (own_part[...] + recv_part[...].astype(F32)) * silu_slope(v)
    upstream = keep_inside(upstream)
    out[...] = upstream
    stat_out[...] = jnp.broadcast_to(column_sums(upstream, upstream * normed)[None], stat_out.shape)


def spatial_back_kernel(population, ids, stat, moments, pre, upstream, own_prm, w, shifts, own_out, send_out, sums_out):
    sums = jnp.sum(stat[:, pl.ds(ids[1], 1)], axis=(0, 1, 2))
    sums_out[...] = sums
    low = norm_back(sums, population, moments, pre, upstream, own_prm[0:1, 256:512])
    fill_shifts(shifts, low, 1)
    acc = None
    for tap in range(9):
        at = LINE * (2 - tap // 3)
        part = dot_nt(shifts[tap % 3, at : at + SPAN], tap_weights(ids, w, tap))
        acc = part if acc is None else acc + part
    acc = squeeze(acc)
    split_cores(ids, [acc[:, n * 128 : (n + 1) * 128] for n in range(4)], own_out, send_out)


def spatial_grad(ids, hid, shifts, held):
    turned = hid[...].T
    depth = held.shape[1]
    for tap in range(9):
        at = LINE * (2 - tap // 3)
        grad = dot(turned, shifts[tap % 3, at : at + SPAN]).astype(BF)
        row = 0
        for p, a, b in tap_segments(tap, depth):
            for h in range(2):
                held[h * PIECES + p, a:b] = grad[row : row + b - a, h * 128 : (h + 1) * 128]
            row += b - a


def reduce_back_kernel(population, ids, stat, moments, pre, upstream, own_prm, w, low_out, own_out, send_out, sums_out):
    sums = jnp.sum(stat[:, pl.ds(ids[1], 1)], axis=(0, 1, 2))
    sums_out[...] = sums
    low = norm_back(sums, population, moments, pre, upstream, own_prm[0:1, 0:256]).astype(BF)
    low_out[...] = low
    core = ids[1]
    for c, dst in ((1 - core, send_out), (core, own_out)):
        for k in range(2):
            for j in range(2):
                p = 2 * (2 * k + c) + j
                part = dot_nt(low, lanes([piece_of(ids, w, 0, p), piece_of(ids, w, 1, p)]))
                at = k * 512 + j * 256
                dst[:, at : at + 256] = part.astype(dst.dtype)


def reduce_grad(ids, xo, xt, low, held):
    core = ids[1]
    for c, src in ((core, xo), (1 - core, xt)):
        grad = dot_tn(src[...], low[...]).astype(BF)
        for k in range(2):
            for j in range(2):
                p = 2 * (2 * k + c) + j
                at = k * 512 + j * 256
                for h in range(2):
                    held[h * PIECES + p] = grad[at : at + 256, h * 128 : (h + 1) * 128]


def leave_kernel(ids, full, keep_out, send_out):
    first = ids[0] == 0
    a = full[:, :512]
    b = full[:, 512:]
    keep_out[...] = jnp.where(first, a, b)
    send_out[...] = jnp.where(first, b, a).astype(BF)


def leave_sum_kernel(ids, outside, own_part, recv_part, keep_out, send_out):
    first = ids[0] == 0
    full = outside[...] + own_part[...] + recv_part[...].astype(F32)
    a = full[:, :512]
    b = full[:, 512:]
    keep_out[...] = jnp.where(first, a, b)
    send_out[...] = jnp.where(first, b, a).astype(BF)


def arrive_kernel(ids, keep, recv, out):
    x = ids[0]
    for src, owner in ((keep, x), (recv, 1 - x)):
        for i in range(NIMG):
            img = src[i * IMG : (i + 1) * IMG].astype(F32).reshape(SIDE, LINE, src.shape[1])
            out[owner * NIMG + i] = img[:, :SIDE, :]


def moments_step(first, second, gradient):
    first_new = FIRST_DECAY * first + (1.0 - FIRST_DECAY) * gradient
    second_new = SECOND_DECAY * second + (1.0 - SECOND_DECAY) * gradient * gradient
    update = (first_new / (1.0 - FIRST_DECAY**STEP)) / (
        jnp.sqrt(second_new / (1.0 - SECOND_DECAY**STEP)) + ADAM_EPSILON
    )
    return second_new, update


def cell(v, lane):
    return jnp.where(lax.broadcasted_iota(jnp.int32, (1, 128), 1) == lane, jnp.sum(v), 0.0)


def lamb_kernel(plans, cuts, lines, arrays, *refs):
    blocks = iter(refs[:arrays])
    refs = refs[arrays:]
    count = sum(len(cut) for cut in cuts)
    masters, firsts, seconds = (refs[i * count : (i + 1) * count] for i in range(3))
    before = refs[3 * count : 3 * count + lines]
    outs = refs[len(refs) - 3 * count - 1 :]
    line = jnp.zeros((1, 128), F32)
    for ref in before:
        line = line + ref[...]
    i = 0
    for plan, cut in zip(plans, cuts):
        total = evaluate(plan, blocks)[0]
        for (b, m), lo, hi in cut:
            grad = total[lo:hi]
            master = masters[i][0]
            if grad.shape != master.shape:
                depth = master.shape[0]
                grad = lanes([grad[n * depth : (n + 1) * depth] for n in range(grad.shape[0] // depth)])
            second_new, update = moments_step(firsts[i][0], seconds[i][0], grad)
            update = update + WEIGHT_DECAY * master
            outs[3 * i][0] = grad
            outs[3 * i + 1][0] = second_new
            outs[3 * i + 2][0] = update
            line = line + cell(master * master, (b * 3 + m) * 2) + cell(update * update, (b * 3 + m) * 2 + 1)
            i += 1
    outs[-1][...] = jnp.broadcast_to(line[None], outs[-1].shape) if len(outs[-1].shape) == 3 else line


def lamb(sources, masters, firsts, seconds, filled, lines, count):
    whole = pl.BlockSpec(memory_space=pltpu.VMEM)
    tasks = [task for task, _ in sources]
    cuts = [cut for _, cut in sources]
    items = [item for cut in cuts for item, _, _ in cut]
    args, specs = slices(tasks, 1, 0)
    arrays = len(args)
    outs, out_specs, aliases = [], [], {}

    def one(b, m):
        return pl.BlockSpec((1,) + masters[m].shape[1:], lambda _: (b, 0, 0))

    for source in (masters, firsts, seconds):
        for b, m in items:
            args.append(source[m])
            specs.append(one(b, m))
    for line in lines:
        args.append(line)
        specs.append(whole)
    for b, m in items:
        for k in range(3):
            if filled[m] is not None:
                aliases[len(args)] = len(outs)
                args.append(filled[m][k])
                specs.append(pl.BlockSpec(memory_space=pl.ANY))
            outs.append(jax.ShapeDtypeStruct(masters[m].shape, F32))
            out_specs.append(one(b, m))
    outs.append(jax.ShapeDtypeStruct((count, 1, 128) if count else (1, 128), F32))
    out_specs.append(whole)
    found = pl.pallas_call(
        functools.partial(lamb_kernel, [task.plan() for task in tasks], cuts, len(lines), arrays),
        out_shape=outs,
        grid=(1,),
        in_specs=specs,
        out_specs=out_specs,
        input_output_aliases=aliases,
        compiler_params=pltpu.CompilerParams(vmem_limit_bytes=16 * 1024 * 1024),
        name="lamb",
    )(*args)
    for i, (b, m) in enumerate(items):
        filled[m] = tuple(found[3 * i : 3 * i + 3])
    return found[-1]


def renew_kernel(blocks, stat, *refs):
    masters, updates, outs, norms_out = refs[0:3], refs[3:6], refs[6:9], refs[9]
    norms = jnp.sqrt(jnp.sum(stat[...], 0))
    norms_out[...] = norms
    for b in range(blocks):
        for m in range(3):
            at = (b * 3 + m) * 2
            ratio = norms[:, at : at + 1] / norms[:, at + 1 : at + 2]
            outs[m][b] = masters[m][b] - MATRIX_RATE * ratio * updates[m][b]


def norm_kernel(blocks, ids, *refs):
    sums = refs[: 3 * blocks]
    params, first, second = refs[3 * blocks : 3 * blocks + 3]
    grads_out, square_out, new_out = refs[3 * blocks + 3 :]
    front = ids[0] == 0
    for b in range(blocks):
        parts = [[], []]
        for n in range(3):
            pair = unpack_rows(sums[3 * b + n][...])
            for kind in range(2):
                v = pair[1 - kind]
                half = v.shape[1] // 2
                parts[kind].append(jnp.where(front, v[:, :half], v[:, half:]))
        for kind in range(2):
            g = lanes(parts[kind])
            second_new, update = moments_step(first[b, kind], second[b, kind], g)
            grads_out[b, kind] = g
            square_out[b, kind] = second_new
            new_out[b, kind] = params[b, kind] - NORM_RATE * update


def exchange(step):
    pairs = []
    for i in range(32):
        core = (i >> 3) & 1
        pairs.append((i, i ^ (4, 2, 16 if core else 1, 1 if core else 16)[step]))
    return pairs


class Gather:
    def __init__(self, held):
        self.parts = (held,)

    def step(self, step, *after):
        if after:
            self.wait(*after)
        held = self.held()
        self.parts = (held, lax.ppermute(held, ALL, exchange(step)))

    def wait(self, *after):
        self.parts = order(self.parts, *after)

    def held(self):
        return self.parts[0] if len(self.parts) == 1 else jnp.concatenate(self.parts, 0)

    def last(self):
        return self.parts[-1]

    def weight(self):
        return list(self.parts), (0, self.parts[0].shape[1])


def order(value, *before):
    return lax.optimization_barrier((value, before))[0]


class Scatter:
    def __init__(self, near=None, far=None, parts=()):
        self.terms = [] if near is None else [near]
        self.far = far
        self.parts = parts

    def wait(self, *after):
        for part in self.parts:
            part.wait(*after)
        if self.terms:
            self.terms = list(order(tuple(self.terms), *after))

    def arrays(self):
        return [array for part in self.parts for array in part.arrays()] + self.terms

    def rows(self):
        return self.terms[0].shape[1] if self.terms else sum(part.rows() for part in self.parts)

    def plan(self):
        return [part.plan() for part in self.parts], len(self.terms)

    def send(self, step, value):
        self.terms.append(lax.ppermute(value, ALL, exchange(step)))


def evaluate(plan, refs):
    parts, count = plan
    found = [jnp.concatenate([evaluate(part, refs) for part in parts], axis=1)] if parts else []
    found += [next(refs)[...].astype(F32) for _ in range(count)]
    return functools.reduce(jnp.add, found)


def slices(tasks, size, at):
    arrays = [array for task in tasks for array in task.arrays()]
    return arrays, [pl.BlockSpec((size,) + array.shape[1:], lambda _: (at, 0, 0)) for array in arrays]


def add_up_kernel(plans, *refs):
    blocks = iter(refs[: len(refs) - len(plans)])
    for plan, out in zip(plans, refs[len(refs) - len(plans) :]):
        out[...] = evaluate(plan, blocks).astype(out.dtype)


def advance_sums(steps, *after):
    arrays, specs, outs, plans = [], [], [], []
    for task, step in steps:
        task.wait(*after)
    for task, step in steps:
        size = 1 << step
        more, blocks = slices([task], size, 1)
        arrays += more
        specs += blocks
        outs.append(jax.ShapeDtypeStruct((size, task.rows(), 128), BF))
        plans.append(task.plan())
    sends = pl.pallas_call(
        functools.partial(add_up_kernel, plans),
        out_shape=outs,
        grid=(1,),
        in_specs=specs,
        out_specs=[pl.BlockSpec(memory_space=pltpu.VMEM)] * len(outs),
        compiler_params=pltpu.CompilerParams(vmem_limit_bytes=16 * 1024 * 1024),
        name="add_up",
    )(*arrays)
    for (task, step), value in zip(steps, sends):
        task.send(step, value)
    return sends


def body(
    wide,
    block_input,
    out_grad,
    conv_reduce,
    conv_spatial,
    conv_expand,
    first_reduce,
    first_spatial,
    first_expand,
    second_reduce,
    second_spatial,
    second_expand,
    norm_params,
    norm_first,
    norm_second,
):
    blocks = conv_reduce.shape[0]
    population = float(block_input.shape[0] * SIDE * SIDE * wide)
    count = 4 * wide
    x = lax.axis_index("x").astype(jnp.int32)
    core = lax.axis_index("core").astype(jnp.int32)
    w = lax.axis_index("wide").astype(jnp.int32)
    fast = wide == PIECES
    here = jnp.stack([x, core, w, jnp.zeros((), jnp.int32)])
    count_up = jnp.arange(2 * PIECES, dtype=jnp.int32)
    ids = jnp.concatenate([here, count_up, count_up])
    to_x = count_up // PIECES
    to_w = count_up % PIECES

    apart_x = to_x ^ x
    apart_w = to_w ^ w
    back = jnp.where(core == 0, apart_w & 1, apart_x)
    front = jnp.where(core == 0, apart_x, apart_w & 1)
    places = front * 8 + back * 4 + ((apart_w & 2) | (apart_w >> 2))
    bit3, bit2 = count_up >> 3, (count_up >> 2) & 1
    from_x = x ^ jnp.where(core == 0, bit3, bit2)
    from_w = w ^ (jnp.where(core == 0, bit2, bit3) | (count_up & 2) | ((count_up & 1) << 2))
    relative = jnp.concatenate([here, places, from_x * PIECES + from_w])

    swap = [(0, 1), (1, 0)]

    def over_core(v):
        return lax.ppermute(v, "core", swap)

    def over_x(v):
        return lax.ppermute(v, "x", swap)

    def share(v, axes):
        return lax.all_to_all(v, axes, 0, 0)

    def run(kernel, outs, *args, places=None, **kw):
        return call(kernel, outs, ids if places is None else places, *args, smem=(0,), **kw)

    wide_row = norm_params.shape[-1]
    near = norm_params.reshape(2 * blocks, wide_row)
    both = jnp.stack([near, over_core(near)])
    far = over_x(both)
    own_all, oth_all = run(
        params_kernel, [((2 * blocks, 2 * wide_row), F32)] * 2, both, far, name="norm_rows"
    )
    own_prm = [own_all[2 * b : 2 * b + 2] for b in range(blocks)]
    oth_prm = [oth_all[2 * b : 2 * b + 2] for b in range(blocks)]

    act = (ROWS, 512)
    keep_x, send_x, keep_g, send_g = run(enter_kernel, [(act, BF)] * 4, block_input, out_grad, name="enter")
    recv_x = over_x(send_x)
    low_stream = stream = run(join_kernel, [((ROWS, 1024), BF)], keep_x, recv_x, name="join")[0]

    def gather(shard, columns):
        whole = lax.all_gather(shard.astype(BF), CROSS, axis=0, tiled=True).reshape(2 * PIECES, -1, columns)
        return [whole], (0, whole.shape[1])

    table = relative if fast else ids
    tables = [table] + [ids] * (blocks - 1)
    gathers = []
    weights = None
    if fast:
        depth = conv_expand.shape[1]

        def shards(b):
            blocked = conv_expand[b].astype(BF).reshape(depth, 4, 128).swapaxes(0, 1).reshape(4 * depth, 128)
            return [conv_reduce[b].astype(BF), conv_spatial[b].astype(BF), blocked]

        gathers = [Gather(shard[None]) for shard in shards(0)]
        gathers[0].step(0, send_x)
        gathers[0].step(1)
        gathers[1].step(0, gathers[0].parts[0])
        gathers[0].step(2, recv_x, far)
        gathers[1].step(1, gathers[0].parts[0])
        gathers[2].step(0, gathers[1].parts[0])
        gathers[2].step(1)
        gathers[0].step(3)
        wholes = [lax.all_gather(jnp.concatenate(shards(b)), CROSS, axis=0, tiled=False) for b in range(1, blocks)]
        one = conv_reduce.shape[1]
        two = one + conv_spatial.shape[1]
        cuts = ((0, one), (one, two), (two, two + 4 * depth))
    else:
        weights = [
            (gather(conv_reduce[b], 128), gather(conv_spatial[b], 128), gather(conv_expand[b], 512)) for b in range(blocks)
        ]

    def weight_of(b, m):
        if not fast:
            return weights[b][m]
        return gathers[m].weight() if b == 0 else ([wholes[b - 1]], cuts[m])

    def advance(stage, stat, out):
        if not fast:
            return
        if stage == 1:
            gathers[1].step(2, out)
            gathers[1].step(3, stat)
        elif stage == 2:
            gathers[2].step(2, gathers[1].last())
            gathers[2].step(3, out)

    inner = (count, 4, 128)
    outer = (2 * wide, 16, 128)
    saved = []
    for b in range(blocks):
        other = over_core(low_stream)
        pre1, low1, stat = run(
            reduce_kernel,
            [((ROWS, 256), F32), ((ROWS, 256), BF), (inner, F32)],
            low_stream,
            other,
            weight=weight_of(b, 0),
            places=tables[b],
            name="reduce",
        )
        low1 = over_core(low1)
        stat = share(stat, ALL)
        advance(3 * b + 1, stat, pre1)
        stat = stat.reshape(2, 2, wide, 4, 128)
        hid1, moments1, pre2, low2, stat = run(
            functools.partial(spatial_kernel, population),
            [((SPAN, 512), BF), ((8, 256), F32), ((ROWS, 256), F32), ((ROWS, 256), BF), (inner, F32)],
            stat,
            pre1,
            low1,
            own_prm[b],
            oth_prm[b],
            weight=weight_of(b, 1),
            scratch=[pltpu.VMEM((3, SPAN + 2 * LINE, 512), BF)],
            places=tables[b],
            name="spatial",
        )
        low2 = over_core(low2)
        if b > 0:
            stat = order(stat, low2)
        stat = share(stat, ALL)
        advance(3 * b + 2, stat, pre2)
        if fast and b == 0:
            stat, *wholes = lax.optimization_barrier((stat, *wholes))
        stat = stat.reshape(2, 2, wide, 4, 128)
        before = stat
        hid2, moments2, pre3, stat = run(
            functools.partial(expand_kernel, population),
            [((ROWS, 512), BF), ((8, 256), F32), ((ROWS, 1024), F32), (outer, F32)],
            stat,
            pre2,
            low2,
            own_prm[b],
            oth_prm[b],
            weight=weight_of(b, 2),
            places=tables[b],
            name="expand",
        )
        if b == blocks - 1:
            recv_g = over_x(order(send_g, before))
        stat = share(stat, CROSS)
        advance(3 * b + 3, stat, pre3)
        item = dict(
            xo=low_stream, xt=other, stream=stream, pre1=pre1, hid1=hid1, m1=moments1, pre2=pre2, hid2=hid2, m2=moments2, pre3=pre3
        )
        if b < blocks - 1:
            item["m3"], stream, low_stream = call(
                functools.partial(close_kernel, population),
                [((8, 1024), F32), ((ROWS, 1024), F32), ((ROWS, 1024), BF)],
                stat,
                pre3,
                stream,
                own_prm[b],
                name="close",
            )
        else:
            item["m3"], result, outside, stat = run(
                functools.partial(last_kernel, population),
                [((8, 1024), F32), ((ROWS, 1024), F32), ((ROWS, 1024), F32), (outer, F32)],
                stat,
                pre3,
                stream,
                own_prm[b],
                keep_g,
                recv_g,
                name="last",
            )
        saved.append(item)

    tasks = {}

    def hook(kind, b, grads):
        if not fast:
            return []
        near, far = grads
        tasks[kind, b] = Scatter(near, far)
        if (kind, b) != ("reduce", 1):
            tasks[kind, b].send(3, far)
        return [far]

    def ahead(kind, b, stat):
        if not fast:
            return stat
        steps = []
        if b == 1 and kind == "spatial":
            stat = order(stat, tasks["expand", 1].terms[-1])
        if b == 0 and kind == "reduce":
            stat = order(stat, *(tasks[name].terms[-1] for name in ("big", ("expand", 0), ("reduce", 1))))
        if b == 1 and kind == "reduce":
            tasks["big"] = Scatter(parts=(tasks["expand", 1], tasks["spatial", 1]))
            steps = [(tasks["big"], 2)]
        if b == 0 and kind == "expand":
            tasks["reduce", 1].send(3, order(tasks["reduce", 1].far, stat))
            steps = [(tasks["big"], 1)]
        if b == 0 and kind == "spatial":
            steps = [(tasks["expand", 0], 2), (tasks["reduce", 1], 2), (tasks["big"], 0)]
        if b == 0 and kind == "reduce":
            steps = [(tasks["spatial", 0], 2)]
        return order(stat, *advance_sums(steps, stat)) if steps else stat

    def whole(task, b, m):
        return task, [((b, m), 0, task.rows())]

    def step_of(sources, last=False):
        line = lamb(sources, masters, firsts, seconds, filled, lines if last else [], count if last else 0)
        lines.append(line)
        return line

    images = []

    def finish_images(full, gate, kernel, name):
        keep, send = run(kernel, [(act, F32), (act, BF)], *order(full, gate), name=name)
        images.extend(run(arrive_kernel, [(block_input.shape, F32)], keep, over_x(send), name="arrive"))
        return send

    def finish():
        small, middle, large = (tasks[kind, 0] for kind in ("expand", "reduce", "spatial"))
        advance_sums([(small, 1), (tasks["reduce", 1], 1)], middle.terms[0])
        leaving = finish_images((result,), middle.terms[0], leave_kernel, "leave")
        big = tasks["big"]
        cut = 4 * conv_expand.shape[1]
        sent = advance_sums([(large, 1)], small.terms[-1], tasks["reduce", 1].terms[-1], leaving)
        rest = Scatter(parts=(small, tasks["reduce", 1]))
        sent = advance_sums([(middle, 2), (rest, 0)], sent)
        finish_images(after, sent[0], leave_sum_kernel, "leave_sum")
        line = step_of([(big, [((1, 2), 0, cut), ((1, 1), cut, big.rows())])])
        sent = advance_sums([(middle, 1)], sent, line, norm_grads)
        sent = advance_sums([(large, 0)], sent, rest.terms[-1])
        advance_sums([(middle, 0)], sent)
        line = step_of([(rest, [((0, 2), 0, cut), ((1, 0), cut, rest.rows())])])
        for task in (large, middle):
            task.wait(line, *images)
        return [[whole(large, 0, 1), whole(middle, 0, 0)]]

    def gradient(b, m, kernel, *args, name):
        parts, (lo, hi) = weight_of(b, m)
        shape = (hi - lo, parts[0].shape[2])
        whole = pltpu.VMEM((2 * PIECES,) + shape, BF)
        half = ((PIECES,) + shape, BF)

        def halves(ids, *refs):
            kernel(ids, *refs[:-3], refs[-1])
            deal(ids, refs[-1], refs[-3], refs[-2])

        return run(halves, [half] * 2, *args, scratch=[whole], places=table, name=name)

    sums = [None] * (3 * blocks)
    local = [None] * blocks
    after = None
    for b in reversed(range(blocks)):
        item = saved[b]
        w_reduce, w_spatial, w_expand = (weight_of(b, m) for m in range(3))
        if after is not None:
            outside, stat = call(
                outer_back_kernel,
                [((ROWS, 1024), F32), (outer, F32)],
                item["m3"],
                item["pre3"],
                item["stream"],
                own_prm[b],
                *after,
                name="outer_back",
            )
        stat = ahead("expand", b, share(stat, CROSS))
        low3, own_part, send, sums[3 * b + 2] = run(
            functools.partial(expand_back_kernel, population),
            [((ROWS, 1024), BF), ((ROWS, 256), F32), ((ROWS, 256), BF), ((16, 128), F32)],
            stat,
            item["m3"],
            item["pre3"],
            outside,
            own_prm[b],
            weight=w_expand,
            places=tables[b],
            name="expand_back",
        )
        recv = over_core(send)
        grad_expand = gradient(b, 2, expand_grad, item["hid2"], low3, name="expand_grad")
        own_part = order(own_part, *grad_expand, *hook("expand", b, grad_expand))
        upstream, stat = call(
            functools.partial(inner_back_kernel, 256),
            [((ROWS, 256), F32), (inner, F32)],
            own_part,
            recv,
            item["m2"],
            item["pre2"],
            own_prm[b],
            name="inner_back",
        )
        stat = ahead("spatial", b, share(stat, ALL)).reshape(2, 2, wide, 4, 128)
        shifts, own_part, send, sums[3 * b + 1] = run(
            functools.partial(spatial_back_kernel, population),
            [((3, SPAN + 2 * LINE, 256), BF), ((ROWS, 256), F32), ((ROWS, 256), BF), ((4, 128), F32)],
            stat,
            item["m2"],
            item["pre2"],
            upstream,
            own_prm[b],
            weight=w_spatial,
            places=tables[b],
            name="spatial_back",
        )
        recv = over_core(send)
        grad_spatial = gradient(b, 1, spatial_grad, item["hid1"], shifts, name="spatial_grad")
        own_part = order(own_part, *grad_spatial, *hook("spatial", b, grad_spatial))
        upstream, stat = call(
            functools.partial(inner_back_kernel, 0),
            [((ROWS, 256), F32), (inner, F32)],
            own_part,
            recv,
            item["m1"],
            item["pre1"],
            own_prm[b],
            name="inner_back",
        )
        stat = ahead("reduce", b, share(stat, ALL)).reshape(2, 2, wide, 4, 128)
        low1, own_part, send, sums[3 * b] = run(
            functools.partial(reduce_back_kernel, population),
            [((ROWS, 256), BF), ((ROWS, 1024), F32), ((ROWS, 1024), BF), ((4, 128), F32)],
            stat,
            item["m1"],
            item["pre1"],
            upstream,
            own_prm[b],
            weight=w_reduce,
            places=tables[b],
            name="reduce_back",
        )
        recv = over_core(send)
        grad_reduce = gradient(b, 0, reduce_grad, item["xo"], item["xt"], low1, name="reduce_grad")
        own_part = order(own_part, *grad_reduce, *hook("reduce", b, grad_reduce))
        after = (outside, own_part, recv)
        local[b] = (grad_reduce, grad_spatial, grad_expand)

    def scatter(pair):
        flat = jnp.concatenate(pair).reshape(-1, pair[0].shape[-1])
        return lax.psum_scatter(flat, CROSS, scatter_dimension=0, tiled=True).astype(F32)

    norm_shape = (norm_params.shape, F32)
    norm_grads, norm_square, norm_new = run(
        functools.partial(norm_kernel, blocks), [norm_shape] * 3, *sums, norm_params, norm_first, norm_second, name="norms"
    )
    masters = (conv_reduce, conv_spatial, conv_expand)
    firsts = (first_reduce, first_spatial, first_expand)
    seconds = (second_reduce, second_spatial, second_expand)
    filled = [None] * 3
    lines = []
    if fast:
        batches = finish()
    else:
        finish_images((result,), after[1], leave_kernel, "leave")
        finish_images(after, after[1], leave_sum_kernel, "leave_sum")
        batches = []
        for b in range(blocks):
            for m in range(3):
                part = scatter(local[b][m])
                batches.append([(Scatter(part[None]), [((b, m), 0, part.shape[0])])])
    for n, sources in enumerate(batches):
        step_of(sources, n == len(batches) - 1)
    block_output, input_grad = images
    gradients = [filled[m][0] for m in range(3)]
    squares = [filled[m][1] for m in range(3)]
    updates = [filled[m][2] for m in range(3)]
    line = order(lines[-1], block_output, input_grad, norm_grads, norm_square, norm_new)
    stat = share(line, ALL)
    shapes = [(m.shape, F32) for m in masters]
    renewed = call(
        functools.partial(renew_kernel, blocks), shapes + [((1, 128), F32)], stat, *masters, *updates, name="renew"
    )
    layer_norms = renewed[3][0, : 6 * blocks].reshape(blocks, 3, 2)
    return (
        block_output,
        input_grad,
        *gradients,
        *squares,
        *renewed[:3],
        norm_grads,
        norm_square,
        norm_new,
        layer_norms,
    )


def solution(mesh):
    wide = mesh.shape["wide"]
    fine = Mesh(np.asarray(mesh.devices).reshape(2, 2, wide), ALL)
    narrow = ("x", "core")
    image = P("wide", None, None, narrow)
    matrix = P(None, "wide", narrow)
    row = P(None, None, narrow, None)
    return jax.shard_map(
        functools.partial(body, wide),
        mesh=fine,
        in_specs=(image,) * 2 + (matrix,) * 9 + (row,) * 3,
        out_specs=(image,) * 2 + (matrix,) * 9 + (row,) * 3 + (P(),),
        check_vma=False,
    )
```

profile of v0, /device:TPU:0, one launch (start us, length us, event | category | flops | bytes accessed | tf_op | source)
XLA Modules:
  0.0 373.8 jit_solution(5114411229067219521)
XLA Ops:
  13.7 2.9 collective-permute-start
  16.7 2.7 collective-permute-start.2
  19.4 4.1 %collective-permute-done.2 = bf16[1,256,128]{2,1,0:T(8,128)(2,1)S(1)} collective-permute-done((bf16[1,256,128]{2,1,0:T(8,128)(2,1)S(1)}, bf16[1,256,128]{2,1,0:T(8,128)(2,1)S(1)}, u32[]{:S(2)}, u32[]{:S(2)}) %collective-permute-start.2) | collective-permute-done | bytes 65568 | tf_op jit(solution)/shard_map/ppermute | solution.py:640
  24.9 4.7 %collective-permute-done.5.refs_2_ = f32[2,4,768]{2,1,0:T(4,128)S(1)} collective-permute-done((f32[2,4,768]{2,1,0:T(4,128)S(1)}, f32[2,4,768]{2,1,0:T(4,128)S(1)}, u32[]{:S(2)}, u32[]{:S(2)}) %collective-permute-start.5) | collective-permute-done | bytes 24608 | tf_op jit(solution)/shard_map/ppermute | solution.py:773
  32.5 3.8 %collective-permute-start.9 = (bf16[1,576,128]{2,1,0:T(8,128)(2,1)}, bf16[1,576,128]{2,1,0:T(8,128)(2,1)S(1)}, u32[]{:S(2)}, u32[]{:S(2)}) collective-permute-start(bf16[1,576,128]{2,1,0:T(8,128)(2,1)} %get-tuple-element.246), channel_id=1, source_target_pairs={{0,4},{1,5},{2,6},{3,7},{4,0},{5,1},{6,2},{7,3},{8,12},{9,13},{10,... | collective-permute-start | bytes 442376 | tf_op jit(solution)/shard_map/ppermute | solution.py:640
  36.4 7.1 %collective-permute-done.9 = bf16[1,576,128]{2,1,0:T(8,128)(2,1)S(1)} collective-permute-done((bf16[1,576,128]{2,1,0:T(8,128)(2,1)}, bf16[1,576,128]{2,1,0:T(8,128)(2,1)S(1)}, u32[]{:S(2)}, u32[]{:S(2)}) %collective-permute-start.9) | collective-permute-done | bytes 147488 | tf_op jit(solution)/shard_map/ppermute | solution.py:640
  46.3 13.4 %collective-permute-done.7.refs_4_.refs_7_ = bf16[8,256,128]{2,1,0:T(8,128)(2,1)S(1)} collective-permute-done((bf16[8,256,128]{2,1,0:T(8,128)(2,1)S(1)}, bf16[8,256,128]{2,1,0:T(8,128)(2,1)S(1)}, u32[]{:S(2)}, u32[]{:S(2)}) %collective-permute-start.7) | collective-permute-done | bytes 524320 | tf_op jit(solution)/shard_map/ppermute | solution.py:640
  64.8 12.1 %all_to_all.65 = f32[32,4,128]{2,1,0:T(4,128)S(1)} all-to-all(f32[32,4,128]{2,1,0:T(4,128)S(1)} %get-tuple-element.240), channel_id=1, replica_groups=mesh['x'=2,'core'=2,'wide'=8] {'x','core','wide'}, dimensions={0} | all-to-all | bytes 131072 | tf_op jit(solution)/shard_map/all_to_all | solution.py:776
  81.7 9.6 %collective-permute-done.14 = bf16[1,256,128]{2,1,0:T(8,128)(2,1)S(1)} collective-permute-done((bf16[1,256,128]{2,1,0:T(8,128)(2,1)S(1)}, bf16[1,256,128]{2,1,0:T(8,128)(2,1)S(1)}, u32[]{:S(2)}, u32[]{:S(2)}) %collective-permute-start.14) | collective-permute-done | bytes 65568 | tf_op jit(solution)/shard_map/ppermute | solution.py:640
  92.3 4.8 %collective-permute-done.15 = bf16[2,256,128]{2,1,0:T(8,128)(2,1)S(1)} collective-permute-done((bf16[2,256,128]{2,1,0:T(8,128)(2,1)S(1)}, bf16[2,256,128]{2,1,0:T(8,128)(2,1)S(1)}, u32[]{:S(2)}, u32[]{:S(2)}) %collective-permute-start.15) | collective-permute-done | bytes 131104 | tf_op jit(solution)/shard_map/ppermute | solution.py:640
  97.1 4.7 %collective-permute-done.12.refs_7_ = bf16[8,576,128]{2,1,0:T(8,128)(2,1)S(1)} collective-permute-done((bf16[8,576,128]{2,1,0:T(8,128)(2,1)S(1)}, bf16[8,576,128]{2,1,0:T(8,128)(2,1)S(1)}, u32[]{:S(2)}, u32[]{:S(2)}) %collective-permute-start.12) | collective-permute-done | bytes 1179680 | tf_op jit(solution)/shard_map/ppermute | solution.py:640
  104.4 2.9 spatial.2
  111.9 11.1 %all_to_all.66 = f32[32,4,128]{2,1,0:T(4,128)S(1)} all-to-all(f32[32,4,128]{2,1,0:T(4,128)S(1)} %get-tuple-element.252), channel_id=1, replica_groups=mesh['x'=2,'core'=2,'wide'=8] {'x','core','wide'}, dimensions={0} | all-to-all | bytes 131072 | tf_op jit(solution)/shard_map/all_to_all | solution.py:776
  124.1 2.4 expand.2
  126.5 10.6 %all_to_all.67.refs_0_ = f32[16,16,128]{2,1,0:T(8,128)S(1)} all-to-all(f32[16,16,128]{2,1,0:T(8,128)S(1)} %get-tuple-element.261), channel_id=1, replica_groups=mesh['x'=2,'core'=2,'wide'=8] {'x','wide'}, dimensions={0} | all-to-all | bytes 262144 | tf_op jit(solution)/shard_map/all_to_all | solution.py:776
  138.0 2.5 collective-permute-done.18.refs_2_
  142.0 9.1 %all_to_all.68 = f32[32,4,128]{2,1,0:T(4,128)S(1)} all-to-all(f32[32,4,128]{2,1,0:T(4,128)S(1)} %get-tuple-element.265), channel_id=1, replica_groups=mesh['x'=2,'core'=2,'wide'=8] {'x','core','wide'}, dimensions={0} | all-to-all | bytes 131072 | tf_op jit(solution)/shard_map/all_to_all | solution.py:776
  151.1 2.6 spatial.3
  155.3 9.2 %all_to_all.69 = f32[32,4,128]{2,1,0:T(4,128)S(1)} all-to-all(f32[32,4,128]{2,1,0:T(4,128)S(1)} %get-tuple-element.270), channel_id=1, replica_groups=mesh['x'=2,'core'=2,'wide'=8] {'x','core','wide'}, dimensions={0} | all-to-all | bytes 131072 | tf_op jit(solution)/shard_map/all_to_all | solution.py:776
  165.2 1.7 expand.3
  166.9 11.8 %all_to_all.70.refs_1_ = f32[16,16,128]{2,1,0:T(8,128)S(1)} all-to-all(f32[16,16,128]{2,1,0:T(8,128)S(1)} %get-tuple-element.272), channel_id=1, replica_groups=mesh['x'=2,'core'=2,'wide'=8] {'x','wide'}, dimensions={0} | all-to-all | bytes 262144 | tf_op jit(solution)/shard_map/all_to_all | solution.py:776
  178.7 1.9 last.1
  180.6 10.5 %all_to_all.71.refs_1_ = f32[16,16,128]{2,1,0:T(8,128)S(1)} all-to-all(f32[16,16,128]{2,1,0:T(8,128)S(1)} %get-tuple-element.281), channel_id=1, replica_groups=mesh['x'=2,'core'=2,'wide'=8] {'x','wide'}, dimensions={0} | all-to-all | bytes 262144 | tf_op jit(solution)/shard_map/all_to_all | solution.py:776
  191.1 1.8 expand_back.2
  197.0 9.4 %all_to_all.72 = f32[32,4,128]{2,1,0:T(4,128)S(1)} all-to-all(f32[32,4,128]{2,1,0:T(4,128)S(1)} %get-tuple-element.291), channel_id=1, replica_groups=mesh['x'=2,'core'=2,'wide'=8] {'x','core','wide'}, dimensions={0} | all-to-all | bytes 131072 | tf_op jit(solution)/shard_map/all_to_all | solution.py:776
  206.4 2.4 spatial_back.2
  208.9 2.1 spatial_grad.2
  213.6 14.6 %all_to_all.73 = f32[32,4,128]{2,1,0:T(4,128)S(1)} all-to-all(f32[32,4,128]{2,1,0:T(4,128)S(1)} %get-tuple-element.302), channel_id=1, replica_groups=mesh['x'=2,'core'=2,'wide'=8] {'x','core','wide'}, dimensions={0} | all-to-all | bytes 131072 | tf_op jit(solution)/shard_map/all_to_all | solution.py:776
  234.2 21.5 %all_to_all.74.refs_1_ = f32[16,16,128]{2,1,0:T(8,128)S(1)} all-to-all(f32[16,16,128]{2,1,0:T(8,128)S(1)} %get-tuple-element.315), channel_id=1, replica_groups=mesh['x'=2,'core'=2,'wide'=8] {'x','wide'}, dimensions={0} | all-to-all | bytes 262144 | tf_op jit(solution)/shard_map/all_to_all | solution.py:776
  256.8 2.1 expand_back.3
  264.0 9.5 %all_to_all.75 = f32[32,4,128]{2,1,0:T(4,128)S(1)} all-to-all(f32[32,4,128]{2,1,0:T(4,128)S(1)} %get-tuple-element.331), channel_id=1, replica_groups=mesh['x'=2,'core'=2,'wide'=8] {'x','core','wide'}, dimensions={0} | all-to-all | bytes 131072 | tf_op jit(solution)/shard_map/all_to_all | solution.py:776
  274.9 2.0 spatial_back.3
  276.9 3.1 spatial_grad.3
  286.1 3.4 all-to-all-start.11
  289.5 7.3 %collective-permute-done.33.refs_6_ = bf16[1,832,128]{2,1,0:T(8,128)(2,1)} collective-permute-done((bf16[1,832,128]{2,1,0:T(8,128)(2,1)}, bf16[1,832,128]{2,1,0:T(8,128)(2,1)}, u32[]{:S(2)}, u32[]{:S(2)}) %collective-permute-start.33) | collective-permute-done | bytes 213024 | tf_op jit(solution)/shard_map/ppermute | solution.py:681
  297.1 6.0 %all-to-all-done.11 = f32[32,4,128]{2,1,0:T(4,128)} async-done(((f32[32,4,128]{2,1,0:T(4,128)}), f32[32,4,128]{2,1,0:T(4,128)}, u32[]{:S(2)}, u32[]{:S(2)}) %all-to-all-start.11) | async-done | bytes 65568 | tf_op jit(solution)/shard_map/all_to_all | solution.py:776
  305.3 1.7 reduce_back.3
  312.7 1.7 collective-permute-start.42
  315.1 3.7 collective-permute-done.41.refs_5_.refs_3_
  324.5 1.7 collective-permute-start.37
  328.2 2.0 collective-permute-start.46
  330.4 2.5 lamb.3
  335.0 3.4 collective-permute-done.46.refs_8_
  338.4 1.8 collective-permute-done.44.refs_3_
  345.4 2.0 lamb.4
  353.7 3.8 %all-to-all-start.12 = ((f32[32,1,128]{2,1,0:T(1,128)}), f32[32,1,128]{2,1,0:T(1,128)S(1)}, u32[]{:S(2)}, u32[]{:S(2)}) async-start(f32[32,1,128]{2,1,0:T(1,128)} %get-tuple-element.447), calls=%async_computation.12 | async-start | bytes 32768 | tf_op jit(solution)/shard_map/all_to_all | solution.py:776
  357.5 3.8 %copy.49 = f32[4,14,14,512]{3,0,2,1:T(4,128)} copy(f32[4,14,14,512]{3,2,1,0:T(8,128)} %copy-done.23) | data formatting | bytes 3211264
  361.4 2.2 copy.50
  (343 shorter events, 96.4 us)
Async XLA Ops:
  7.2 115.8 %all-gather.3.cloned.1.call-start = ((), (), s32[]{:S(2)}) async-start(), calls=%async_computation.13 | async-start | bytes 4734976 | tf_op jit(solution)/shard_map/all_gather | solution.py:820
  13.7 16.5 %collective-permute-start = (bf16[448,512]{1,0:T(8,128)(2,1)S(1)}, bf16[448,512]{1,0:T(8,128)(2,1)S(1)}, u32[]{:S(2)}, u32[]{:S(2)}) collective-permute-start(bf16[448,512]{1,0:T(8,128)(2,1)S(1)} %get-tuple-element.236), channel_id=1, source_target_pairs={{0,16},{16,0},{1,17},{17,1},{2,18},{18,2},{3,19},{19,3},{4,20},{20... | collective-permute-start | bytes 1376264 | tf_op jit(solution)/shard_map/ppermute | solution.py:773
  16.7 7.7 %collective-permute-start.4 = (f32[4,768]{1,0:T(4,128)S(1)}, f32[4,768]{1,0:T(4,128)S(1)}, u32[]{:S(2)}, u32[]{:S(2)}) collective-permute-start(f32[4,768]{1,0:T(4,128)S(1)} %reshape.68), channel_id=1, source_target_pairs={{0,8},{8,0},{1,9},{9,1},{2,10},{10,2},{3,11},{11,3},{4,12},{12,4},... | collective-permute-start | bytes 36872 | tf_op jit(solution)/shard_map/ppermute | solution.py:770
  16.7 6.8 %collective-permute-start.2 = (bf16[1,256,128]{2,1,0:T(8,128)(2,1)S(1)}, bf16[1,256,128]{2,1,0:T(8,128)(2,1)S(1)}, u32[]{:S(2)}, u32[]{:S(2)}) collective-permute-start(bf16[1,256,128]{2,1,0:T(8,128)(2,1)S(1)} %get-tuple-element.237), channel_id=1, source_target_pairs={{0,4},{1,5},{2,6},{3,7},{4,0},{5,1},{6,2},{7,3},{8,12},{9,13},{10,... | collective-permute-start | bytes 196616 | tf_op jit(solution)/shard_map/ppermute | solution.py:640
  23.6 6.6 %collective-permute-start.3 = (bf16[2,256,128]{2,1,0:T(8,128)(2,1)S(1)}, bf16[2,256,128]{2,1,0:T(8,128)(2,1)S(1)}, u32[]{:S(2)}, u32[]{:S(2)}) collective-permute-start(bf16[2,256,128]{2,1,0:T(8,128)(2,1)S(1)} %constant_dynamic-update-slice_fusion), channel_id=1, source_target_pairs={{0,2},{1,3},{2,0},{3,1},{4,6},{5,7},{6,4},{7,5},{8,10},{9,11},{10,... | collective-permute-start | bytes 393224 | tf_op jit(solution)/shard_map/ppermute | solution.py:640
  24.3 5.3 %collective-permute-start.5 = (f32[2,4,768]{2,1,0:T(4,128)S(1)}, f32[2,4,768]{2,1,0:T(4,128)S(1)}, u32[]{:S(2)}, u32[]{:S(2)}) collective-permute-start(f32[2,4,768]{2,1,0:T(4,128)S(1)} %pad_maximum_fusion.1.refs_1_), channel_id=1, source_target_pairs={{0,16},{16,0},{1,17},{17,1},{2,18},{18,2},{3,19},{19,3},{4,20},{20... | collective-permute-start | bytes 73736 | tf_op jit(solution)/shard_map/ppermute | solution.py:773
  30.8 28.9 %collective-permute-start.1 = (bf16[448,1024]{1,0:T(8,128)(2,1)S(1)}, bf16[448,1024]{1,0:T(8,128)(2,1)S(1)}, u32[]{:S(2)}, u32[]{:S(2)}) collective-permute-start(bf16[448,1024]{1,0:T(8,128)(2,1)S(1)} %join.1.refs_1_.refs_2_), channel_id=1, source_target_pairs={{0,8},{8,0},{1,9},{9,1},{2,10},{10,2},{3,11},{11,3},{4,12},{12,4},... | collective-permute-start | bytes 2752520 | tf_op jit(solution)/shard_map/ppermute | solution.py:770
  31.0 12.5 %collective-permute-start.6 = (bf16[4,256,128]{2,1,0:T(8,128)(2,1)S(1)}, bf16[4,256,128]{2,1,0:T(8,128)(2,1)S(1)}, u32[]{:S(2)}, u32[]{:S(2)}) collective-permute-start(bf16[4,256,128]{2,1,0:T(8,128)(2,1)S(1)} %get-tuple-element.491), channel_id=1, source_target_pairs={{0,1},{1,0},{2,3},{3,2},{4,5},{5,4},{6,7},{7,6},{8,24},{9,25},{10,... | collective-permute-start | bytes 786440 | tf_op jit(solution)/shard_map/ppermute | solution.py:640
  32.5 10.9 %collective-permute-start.9 = (bf16[1,576,128]{2,1,0:T(8,128)(2,1)}, bf16[1,576,128]{2,1,0:T(8,128)(2,1)S(1)}, u32[]{:S(2)}, u32[]{:S(2)}) collective-permute-start(bf16[1,576,128]{2,1,0:T(8,128)(2,1)} %get-tuple-element.246), channel_id=1, source_target_pairs={{0,4},{1,5},{2,6},{3,7},{4,0},{5,1},{6,2},{7,3},{8,12},{9,13},{10,... | collective-permute-start | bytes 442376 | tf_op jit(solution)/shard_map/ppermute | solution.py:640
  43.5 16.2 %collective-permute-start.7 = (bf16[8,256,128]{2,1,0:T(8,128)(2,1)S(1)}, bf16[8,256,128]{2,1,0:T(8,128)(2,1)S(1)}, u32[]{:S(2)}, u32[]{:S(2)}) collective-permute-start(bf16[8,256,128]{2,1,0:T(8,128)(2,1)S(1)} %constant_dynamic-update-slice_fusion.4.refs_3_.refs_6_), channel_id=1, source_target_pairs={{0,16},{1,17},{2,18},{3,19},{4,20},{5,21},{6,22},{7,23},{8,9},{9,8... | collective-permute-start | bytes 1572872 | tf_op jit(solution)/shard_map/ppermute | solution.py:640
  46.2 14.9 %collective-permute-start.10 = (bf16[2,576,128]{2,1,0:T(8,128)(2,1)}, bf16[2,576,128]{2,1,0:T(8,128)(2,1)}, u32[]{:S(2)}, u32[]{:S(2)}) collective-permute-start(bf16[2,576,128]{2,1,0:T(8,128)(2,1)} %constant_dynamic-update-slice_fusion.7), channel_id=1, source_target_pairs={{0,2},{1,3},{2,0},{3,1},{4,6},{5,7},{6,4},{7,5},{8,10},{9,11},{10,... | collective-permute-start | bytes 884744 | tf_op jit(solution)/shard_map/ppermute | solution.py:640
  63.3 13.6 %collective-permute-start.11 = (bf16[4,576,128]{2,1,0:T(8,128)(2,1)S(1)}, bf16[4,576,128]{2,1,0:T(8,128)(2,1)S(1)}, u32[]{:S(2)}, u32[]{:S(2)}) collective-permute-start(bf16[4,576,128]{2,1,0:T(8,128)(2,1)S(1)} %constant_dynamic-update-slice_fusion.9), channel_id=1, source_target_pairs={{0,1},{1,0},{2,3},{3,2},{4,5},{5,4},{6,7},{7,6},{8,24},{9,25},{10,... | collective-permute-start | bytes 1769480 | tf_op jit(solution)/shard_map/ppermute | solution.py:640
  77.1 24.7 %collective-permute-start.12 = (bf16[8,576,128]{2,1,0:T(8,128)(2,1)S(1)}, bf16[8,576,128]{2,1,0:T(8,128)(2,1)S(1)}, u32[]{:S(2)}, u32[]{:S(2)}) collective-permute-start(bf16[8,576,128]{2,1,0:T(8,128)(2,1)S(1)} %constant_dynamic-update-slice_fusion.11.refs_6_), channel_id=1, source_target_pairs={{0,16},{1,17},{2,18},{3,19},{4,20},{5,21},{6,22},{7,23},{8,9},{9,8... | collective-permute-start | bytes 3538952 | tf_op jit(solution)/shard_map/ppermute | solution.py:640
  80.5 10.7 %collective-permute-start.14 = (bf16[1,256,128]{2,1,0:T(8,128)(2,1)S(1)}, bf16[1,256,128]{2,1,0:T(8,128)(2,1)S(1)}, u32[]{:S(2)}, u32[]{:S(2)}) collective-permute-start(bf16[1,256,128]{2,1,0:T(8,128)(2,1)S(1)} %bitcast.37), channel_id=1, source_target_pairs={{0,4},{1,5},{2,6},{3,7},{4,0},{5,1},{6,2},{7,3},{8,12},{9,13},{10,... | collective-permute-start | bytes 196616 | tf_op jit(solution)/shard_map/ppermute | solution.py:640
  91.2 5.8 %collective-permute-start.15 = (bf16[2,256,128]{2,1,0:T(8,128)(2,1)S(1)}, bf16[2,256,128]{2,1,0:T(8,128)(2,1)S(1)}, u32[]{:S(2)}, u32[]{:S(2)}) collective-permute-start(bf16[2,256,128]{2,1,0:T(8,128)(2,1)S(1)} %constant_dynamic-update-slice_fusion.13), channel_id=1, source_target_pairs={{0,2},{1,3},{2,0},{3,1},{4,6},{5,7},{6,4},{7,5},{8,10},{9,11},{10,... | collective-permute-start | bytes 393224 | tf_op jit(solution)/shard_map/ppermute | solution.py:640
  91.9 11.5 %collective-permute-start.8 = (bf16[448,256]{1,0:T(8,128)(2,1)}, bf16[448,256]{1,0:T(8,128)(2,1)S(1)}, u32[]{:S(2)}, u32[]{:S(2)}) collective-permute-start(bf16[448,256]{1,0:T(8,128)(2,1)} %copy-done.87), channel_id=1, source_target_pairs={{0,8},{8,0},{1,9},{9,1},{2,10},{10,2},{3,11},{11,3},{4,12},{12,4},... | collective-permute-start | bytes 688136 | tf_op jit(solution)/shard_map/ppermute | solution.py:770
  101.8 7.0 %collective-permute-start.16 = (bf16[4,256,128]{2,1,0:T(8,128)(2,1)S(1)}, bf16[4,256,128]{2,1,0:T(8,128)(2,1)S(1)}, u32[]{:S(2)}, u32[]{:S(2)}) collective-permute-start(bf16[4,256,128]{2,1,0:T(8,128)(2,1)S(1)} %constant_dynamic-update-slice_fusion.15), channel_id=1, source_target_pairs={{0,1},{1,0},{2,3},{3,2},{4,5},{5,4},{6,7},{7,6},{8,24},{9,25},{10,... | collective-permute-start | bytes 786440 | tf_op jit(solution)/shard_map/ppermute | solution.py:640
  110.3 12.8 %collective-permute-start.17 = (bf16[8,256,128]{2,1,0:T(8,128)(2,1)}, bf16[8,256,128]{2,1,0:T(8,128)(2,1)}, u32[]{:S(2)}, u32[]{:S(2)}) collective-permute-start(bf16[8,256,128]{2,1,0:T(8,128)(2,1)} %constant_dynamic-update-slice_fusion.17.refs_6_), channel_id=1, source_target_pairs={{0,16},{1,17},{2,18},{3,19},{4,20},{5,21},{6,22},{7,23},{8,9},{9,8... | collective-permute-start | bytes 1572872 | tf_op jit(solution)/shard_map/ppermute | solution.py:640
  110.9 12.1 %collective-permute-start.13 = (bf16[448,256]{1,0:T(8,128)(2,1)}, bf16[448,256]{1,0:T(8,128)(2,1)}, u32[]{:S(2)}, u32[]{:S(2)}) collective-permute-start(bf16[448,256]{1,0:T(8,128)(2,1)} %get-tuple-element.255), channel_id=1, source_target_pairs={{0,8},{8,0},{1,9},{9,1},{2,10},{10,2},{3,11},{11,3},{4,12},{12,4},... | collective-permute-start | bytes 688136 | tf_op jit(solution)/shard_map/ppermute | solution.py:770
  141.8 9.3 %collective-permute-start.19 = (bf16[448,256]{1,0:T(8,128)(2,1)S(1)}, bf16[448,256]{1,0:T(8,128)(2,1)S(1)}, u32[]{:S(2)}, u32[]{:S(2)}) collective-permute-start(bf16[448,256]{1,0:T(8,128)(2,1)S(1)} %get-tuple-element.267), channel_id=1, source_target_pairs={{0,8},{8,0},{1,9},{9,1},{2,10},{10,2},{3,11},{11,3},{4,12},{12,4},... | collective-permute-start | bytes 688136 | tf_op jit(solution)/shard_map/ppermute | solution.py:770
  164.5 14.2 %collective-permute-start.21 = (bf16[448,512]{1,0:T(8,128)(2,1)S(1)}, bf16[448,512]{1,0:T(8,128)(2,1)S(1)}, u32[]{:S(2)}, u32[]{:S(2)}) collective-permute-start(bf16[448,512]{1,0:T(8,128)(2,1)S(1)} %copy-done.86), channel_id=1, source_target_pairs={{0,16},{16,0},{1,17},{17,1},{2,18},{18,2},{3,19},{19,3},{4,20},{20... | collective-permute-start | bytes 1376264 | tf_op jit(solution)/shard_map/ppermute | solution.py:773
  194.3 12.1 %collective-permute-start.23 = (bf16[8,256,128]{2,1,0:T(8,128)(2,1)S(1)}, bf16[8,256,128]{2,1,0:T(8,128)(2,1)S(1)}, u32[]{:S(2)}, u32[]{:S(2)}) collective-permute-start(bf16[8,256,128]{2,1,0:T(8,128)(2,1)S(1)} %get-tuple-element.287), channel_id=1, source_target_pairs={{0,16},{1,17},{2,18},{3,19},{4,20},{5,21},{6,22},{7,23},{8,9},{9,8... | collective-permute-start | bytes 1572872 | tf_op jit(solution)/shard_map/ppermute | solution.py:681
  211.0 17.1 %collective-permute-start.25 = (bf16[8,576,128]{2,1,0:T(8,128)(2,1)S(1)}, bf16[8,576,128]{2,1,0:T(8,128)(2,1)S(1)}, u32[]{:S(2)}, u32[]{:S(2)}) collective-permute-start(bf16[8,576,128]{2,1,0:T(8,128)(2,1)S(1)} %get-tuple-element.298), channel_id=1, source_target_pairs={{0,16},{1,17},{2,18},{3,19},{4,20},{5,21},{6,22},{7,23},{8,9},{9,8... | collective-permute-start | bytes 3538952 | tf_op jit(solution)/shard_map/ppermute | solution.py:681
  229.8 2.9 collective-permute-start.26
  230.0 25.7 %collective-permute-start.27 = (bf16[4,832,128]{2,1,0:T(8,128)(2,1)S(1)}, bf16[4,832,128]{2,1,0:T(8,128)(2,1)S(1)}, u32[]{:S(2)}, u32[]{:S(2)}) collective-permute-start(bf16[4,832,128]{2,1,0:T(8,128)(2,1)S(1)} %add_up.10), channel_id=1, source_target_pairs={{0,1},{1,0},{2,3},{3,2},{4,5},{5,4},{6,7},{7,6},{8,24},{9,25},{10,... | collective-permute-start | bytes 2555912 | tf_op jit(solution)/shard_map/ppermute | solution.py:681
  255.9 17.6 %collective-permute-start.30 = (bf16[8,256,128]{2,1,0:T(8,128)(2,1)S(1)}, bf16[8,256,128]{2,1,0:T(8,128)(2,1)S(1)}, u32[]{:S(2)}, u32[]{:S(2)}) collective-permute-start(bf16[8,256,128]{2,1,0:T(8,128)(2,1)S(1)} %get-tuple-element.334), channel_id=1, source_target_pairs={{0,16},{1,17},{2,18},{3,19},{4,20},{5,21},{6,22},{7,23},{8,9},{9,8... | collective-permute-start | bytes 1572872 | tf_op jit(solution)/shard_map/ppermute | solution.py:681
  260.2 13.3 %collective-permute-start.29 = (bf16[8,256,128]{2,1,0:T(8,128)(2,1)S(1)}, bf16[8,256,128]{2,1,0:T(8,128)(2,1)S(1)}, u32[]{:S(2)}, u32[]{:S(2)}) collective-permute-start(bf16[8,256,128]{2,1,0:T(8,128)(2,1)S(1)} %get-tuple-element.327), channel_id=1, source_target_pairs={{0,16},{1,17},{2,18},{3,19},{4,20},{5,21},{6,22},{7,23},{8,9},{9,8... | collective-permute-start | bytes 1572872 | tf_op jit(solution)/shard_map/ppermute | solution.py:681
  261.5 12.0 %collective-permute-start.31 = (bf16[2,832,128]{2,1,0:T(8,128)(2,1)S(1)}, bf16[2,832,128]{2,1,0:T(8,128)(2,1)S(1)}, u32[]{:S(2)}, u32[]{:S(2)}) collective-permute-start(bf16[2,832,128]{2,1,0:T(8,128)(2,1)S(1)} %add_up.11), channel_id=1, source_target_pairs={{0,2},{1,3},{2,0},{3,1},{4,6},{5,7},{6,4},{7,5},{8,10},{9,11},{10,... | collective-permute-start | bytes 1277960 | tf_op jit(solution)/shard_map/ppermute | solution.py:681
  280.0 23.1 %collective-permute-start.36 = (bf16[8,576,128]{2,1,0:T(8,128)(2,1)}, bf16[8,576,128]{2,1,0:T(8,128)(2,1)S(1)}, u32[]{:S(2)}, u32[]{:S(2)}) collective-permute-start(bf16[8,576,128]{2,1,0:T(8,128)(2,1)} %get-tuple-element.352), channel_id=1, source_target_pairs={{0,16},{1,17},{2,18},{3,19},{4,20},{5,21},{6,22},{7,23},{8,9},{9,8... | collective-permute-start | bytes 3538952 | tf_op jit(solution)/shard_map/ppermute | solution.py:681
  281.5 2.8 collective-permute-start.32
  281.5 15.2 %collective-permute-start.34 = (bf16[4,256,128]{2,1,0:T(8,128)(2,1)}, bf16[4,256,128]{2,1,0:T(8,128)(2,1)S(1)}, u32[]{:S(2)}, u32[]{:S(2)}) collective-permute-start(bf16[4,256,128]{2,1,0:T(8,128)(2,1)} %get-tuple-element.343), channel_id=1, source_target_pairs={{0,1},{1,0},{2,3},{3,2},{4,5},{5,4},{6,7},{7,6},{8,24},{9,25},{10,... | collective-permute-start | bytes 786440 | tf_op jit(solution)/shard_map/ppermute | solution.py:681
  282.3 14.9 %collective-permute-start.35 = (bf16[4,256,128]{2,1,0:T(8,128)(2,1)}, bf16[4,256,128]{2,1,0:T(8,128)(2,1)}, u32[]{:S(2)}, u32[]{:S(2)}) collective-permute-start(bf16[4,256,128]{2,1,0:T(8,128)(2,1)} %get-tuple-element.344), channel_id=1, source_target_pairs={{0,1},{1,0},{2,3},{3,2},{4,5},{5,4},{6,7},{7,6},{8,24},{9,25},{10,... | collective-permute-start | bytes 786440 | tf_op jit(solution)/shard_map/ppermute | solution.py:681
  283.5 13.2 %collective-permute-start.33 = (bf16[1,832,128]{2,1,0:T(8,128)(2,1)}, bf16[1,832,128]{2,1,0:T(8,128)(2,1)}, u32[]{:S(2)}, u32[]{:S(2)}) collective-permute-start(bf16[1,832,128]{2,1,0:T(8,128)(2,1)} %get-tuple-element.345), channel_id=1, source_target_pairs={{0,4},{1,5},{2,6},{3,7},{4,0},{5,1},{6,2},{7,3},{8,12},{9,13},{10,... | collective-permute-start | bytes 638984 | tf_op jit(solution)/shard_map/ppermute | solution.py:681
  286.1 17.1 %all-to-all-start.11 = ((f32[32,4,128]{2,1,0:T(4,128)}), f32[32,4,128]{2,1,0:T(4,128)}, u32[]{:S(2)}, u32[]{:S(2)}) async-start(f32[32,4,128]{2,1,0:T(4,128)} %copy-done.67), calls=%async_computation.11 | async-start | bytes 131072 | tf_op jit(solution)/shard_map/all_to_all | solution.py:776
  307.0 19.2 %collective-permute-start.38 = (bf16[448,1024]{1,0:T(8,128)(2,1)S(1)}, bf16[448,1024]{1,0:T(8,128)(2,1)S(1)}, u32[]{:S(2)}, u32[]{:S(2)}) collective-permute-start(bf16[448,1024]{1,0:T(8,128)(2,1)S(1)} %get-tuple-element.370), channel_id=1, source_target_pairs={{0,8},{8,0},{1,9},{9,1},{2,10},{10,2},{3,11},{11,3},{4,12},{12,4},... | collective-permute-start | bytes 2752520 | tf_op jit(solution)/shard_map/ppermute | solution.py:770
  307.2 14.1 %collective-permute-start.40 = (bf16[4,576,128]{2,1,0:T(8,128)(2,1)S(1)}, bf16[4,576,128]{2,1,0:T(8,128)(2,1)S(1)}, u32[]{:S(2)}, u32[]{:S(2)}) collective-permute-start(bf16[4,576,128]{2,1,0:T(8,128)(2,1)S(1)} %add_up.13), channel_id=1, source_target_pairs={{0,1},{1,0},{2,3},{3,2},{4,5},{5,4},{6,7},{7,6},{8,24},{9,25},{10,... | collective-permute-start | bytes 1769480 | tf_op jit(solution)/shard_map/ppermute | solution.py:681
  309.8 12.3 %collective-permute-start.39 = (bf16[8,256,128]{2,1,0:T(8,128)(2,1)S(1)}, bf16[8,256,128]{2,1,0:T(8,128)(2,1)S(1)}, u32[]{:S(2)}, u32[]{:S(2)}) collective-permute-start(bf16[8,256,128]{2,1,0:T(8,128)(2,1)S(1)} %get-tuple-element.368), channel_id=1, source_target_pairs={{0,16},{1,17},{2,18},{3,19},{4,20},{5,21},{6,22},{7,23},{8,9},{9,8... | collective-permute-start | bytes 1572872 | tf_op jit(solution)/shard_map/ppermute | solution.py:681
  312.4 6.5 %collective-permute-start.41 = (bf16[2,256,128]{2,1,0:T(8,128)(2,1)S(1)}, bf16[2,256,128]{2,1,0:T(8,128)(2,1)S(1)}, u32[]{:S(2)}, u32[]{:S(2)}) collective-permute-start(bf16[2,256,128]{2,1,0:T(8,128)(2,1)S(1)} %get-tuple-element.377), channel_id=1, source_target_pairs={{0,2},{1,3},{2,0},{3,1},{4,6},{5,7},{6,4},{7,5},{8,10},{9,11},{10,... | collective-permute-start | bytes 393224 | tf_op jit(solution)/shard_map/ppermute | solution.py:681
  312.7 7.8 %collective-permute-start.42 = (bf16[2,256,128]{2,1,0:T(8,128)(2,1)S(1)}, bf16[2,256,128]{2,1,0:T(8,128)(2,1)S(1)}, u32[]{:S(2)}, u32[]{:S(2)}) collective-permute-start(bf16[2,256,128]{2,1,0:T(8,128)(2,1)S(1)} %get-tuple-element.378), channel_id=1, source_target_pairs={{0,2},{1,3},{2,0},{3,1},{4,6},{5,7},{6,4},{7,5},{8,10},{9,11},{10,... | collective-permute-start | bytes 393224 | tf_op jit(solution)/shard_map/ppermute | solution.py:681
  323.2 10.9 %collective-permute-start.45 = (bf16[4,256,128]{2,1,0:T(8,128)(2,1)S(1)}, bf16[4,256,128]{2,1,0:T(8,128)(2,1)S(1)}, u32[]{:S(2)}, u32[]{:S(2)}) collective-permute-start(bf16[4,256,128]{2,1,0:T(8,128)(2,1)S(1)} %get-tuple-element.392), channel_id=1, source_target_pairs={{0,1},{1,0},{2,3},{3,2},{4,5},{5,4},{6,7},{7,6},{8,24},{9,25},{10,... | collective-permute-start | bytes 786440 | tf_op jit(solution)/shard_map/ppermute | solution.py:681
  324.5 18.9 %collective-permute-start.37 = (bf16[448,512]{1,0:T(8,128)(2,1)S(1)}, bf16[448,512]{1,0:T(8,128)(2,1)S(1)}, u32[]{:S(2)}, u32[]{:S(2)}) collective-permute-start(bf16[448,512]{1,0:T(8,128)(2,1)S(1)} %get-tuple-element.366), channel_id=1, source_target_pairs={{0,16},{16,0},{1,17},{17,1},{2,18},{18,2},{3,19},{19,3},{4,20},{20... | collective-permute-start | bytes 1376264 | tf_op jit(solution)/shard_map/ppermute | solution.py:773
  327.1 20.7 %collective-permute-start.43 = (bf16[448,512]{1,0:T(8,128)(2,1)S(1)}, bf16[448,512]{1,0:T(8,128)(2,1)S(1)}, u32[]{:S(2)}, u32[]{:S(2)}) collective-permute-start(bf16[448,512]{1,0:T(8,128)(2,1)S(1)} %get-tuple-element.397), channel_id=1, source_target_pairs={{0,16},{16,0},{1,17},{17,1},{2,18},{18,2},{3,19},{19,3},{4,20},{20... | collective-permute-start | bytes 1376264 | tf_op jit(solution)/shard_map/ppermute | solution.py:773
  327.5 12.7 %collective-permute-start.44 = (bf16[2,576,128]{2,1,0:T(8,128)(2,1)S(1)}, bf16[2,576,128]{2,1,0:T(8,128)(2,1)S(1)}, u32[]{:S(2)}, u32[]{:S(2)}) collective-permute-start(bf16[2,576,128]{2,1,0:T(8,128)(2,1)S(1)} %add_up.15), channel_id=1, source_target_pairs={{0,2},{1,3},{2,0},{3,1},{4,6},{5,7},{6,4},{7,5},{8,10},{9,11},{10,... | collective-permute-start | bytes 884744 | tf_op jit(solution)/shard_map/ppermute | solution.py:681
  328.2 10.1 %collective-permute-start.46 = (bf16[1,512,128]{2,1,0:T(8,128)(2,1)S(1)}, bf16[1,512,128]{2,1,0:T(8,128)(2,1)S(1)}, u32[]{:S(2)}, u32[]{:S(2)}) collective-permute-start(bf16[1,512,128]{2,1,0:T(8,128)(2,1)S(1)} %get-tuple-element.398), channel_id=1, source_target_pairs={{0,4},{1,5},{2,6},{3,7},{4,0},{5,1},{6,2},{7,3},{8,12},{9,13},{10,... | collective-permute-start | bytes 393224 | tf_op jit(solution)/shard_map/ppermute | solution.py:681
  334.2 8.5 %collective-permute-start.48 = (bf16[2,256,128]{2,1,0:T(8,128)(2,1)S(1)}, bf16[2,256,128]{2,1,0:T(8,128)(2,1)S(1)}, u32[]{:S(2)}, u32[]{:S(2)}) collective-permute-start(bf16[2,256,128]{2,1,0:T(8,128)(2,1)S(1)} %add_up.17), channel_id=1, source_target_pairs={{0,2},{1,3},{2,0},{3,1},{4,6},{5,7},{6,4},{7,5},{8,10},{9,11},{10,... | collective-permute-start | bytes 393224 | tf_op jit(solution)/shard_map/ppermute | solution.py:681
  340.3 10.3 %collective-permute-start.47 = (bf16[1,576,128]{2,1,0:T(8,128)(2,1)S(1)}, bf16[1,576,128]{2,1,0:T(8,128)(2,1)S(1)}, u32[]{:S(2)}, u32[]{:S(2)}) collective-permute-start(bf16[1,576,128]{2,1,0:T(8,128)(2,1)S(1)} %add_up.18), channel_id=1, source_target_pairs={{0,4},{1,5},{2,6},{3,7},{4,0},{5,1},{6,2},{7,3},{8,12},{9,13},{10,... | collective-permute-start | bytes 442376 | tf_op jit(solution)/shard_map/ppermute | solution.py:681
  342.7 7.9 %collective-permute-start.49 = (bf16[1,256,128]{2,1,0:T(8,128)(2,1)S(1)}, bf16[1,256,128]{2,1,0:T(8,128)(2,1)S(1)}, u32[]{:S(2)}, u32[]{:S(2)}) collective-permute-start(bf16[1,256,128]{2,1,0:T(8,128)(2,1)S(1)} %add_up.19), channel_id=1, source_target_pairs={{0,4},{1,5},{2,6},{3,7},{4,0},{5,1},{6,2},{7,3},{8,12},{9,13},{10,... | collective-permute-start | bytes 196616 | tf_op jit(solution)/shard_map/ppermute | solution.py:681
  353.7 10.9 %all-to-all-start.12 = ((f32[32,1,128]{2,1,0:T(1,128)}), f32[32,1,128]{2,1,0:T(1,128)S(1)}, u32[]{:S(2)}, u32[]{:S(2)}) async-start(f32[32,1,128]{2,1,0:T(1,128)} %get-tuple-element.447), calls=%async_computation.12 | async-start | bytes 32768 | tf_op jit(solution)/shard_map/all_to_all | solution.py:776
  (96 other events, 1083.9 us)
Sparse Core Ops, SparseCore 0:
  11.7 94.4 all-gather.2
where the time goes:
time: 377 us; the launch traced here: 374 us
  blocking collectives  129 us (34%)
  waiting for transfers between devices  86.1 us (23%)
  Pallas kernels  57.5 us (15%)
  starting transfers between devices  53.8 us (14%)
  local copies, waits for them, and re-layouts  28.5 us (8%)
  between operations  15.5 us (4%)
    all_to_all x11, blocking collectives, share(): return lax.all_to_all(v, axes, 0, 0)  129 us
    pallas_call x34, Pallas kernels, call(): pl.pallas_call(whole, out_shape=[jax.ShapeDtypeStruct(shape, dtype) for s...  47.2 us
    ppermute x12, waiting for transfers between devices, step(): self.parts = (held, lax.ppermute(held, ALL, exchange(step)))  44.2 us
    unnamed x195, local copies, waits for them, and re-layouts  21.9 us
    ppermute x20, starting transfers between devices, send(): self.terms.append(lax.ppermute(value, ALL, exchange(step)))  21.7 us
    ppermute x20, waiting for transfers between devices, send(): self.terms.append(lax.ppermute(value, ALL, exchange(step)))  21.5 us
    ppermute x12, starting transfers between devices, step(): self.parts = (held, lax.ppermute(held, ALL, exchange(step)))  16.2 us
    ppermute x13, waiting for transfers between devices, over_core(): return lax.ppermute(v, 'core', swap)  8.31 us
  transfers between devices with their start and end apart: 53, of which 26 were waited for; matrix products, arithmetic and copies ran while one was open for 4% of the time, Pallas kernels for 7%

commit v1 on v0

--- a/solution.py
+++ b/solution.py
@@ -858,6 +858,8 @@
         low1 = over_core(low1)
         stat = share(stat, ALL)
         advance(3 * b + 1, stat, pre1)
+        if fast and b == 0:
+            stat, *wholes = lax.optimization_barrier((stat, *wholes))
         stat = stat.reshape(2, 2, wide, 4, 128)
         hid1, moments1, pre2, low2, stat = run(
             functools.partial(spatial_kernel, population),
@@ -877,8 +879,6 @@
             stat = order(stat, low2)
         stat = share(stat, ALL)
         advance(3 * b + 2, stat, pre2)
-        if fast and b == 0:
-            stat, *wholes = lax.optimization_barrier((stat, *wholes))
         stat = stat.reshape(2, 2, wide, 4, 128)
         before = stat
         hid2, moments2, pre3, stat = run(

time: 377 us -> 376 us (level)
    unnamed x195 -> x183, local copies, waits for them, and re-layouts: 21.9 us -> 20.2 us
  transfers between devices with their start and end apart: 53 -> 53, of which waited for: 26 -> 27; matrix products, arithmetic and copies ran while one was open for 4% -> 4% of each run, Pallas kernels for 7% -> 7%
where the time goes in v1:
time: 376 us; the launch traced here: 373 us
  blocking collectives  129 us (34%)
  waiting for transfers between devices  87.7 us (23%)
  Pallas kernels  55.7 us (15%)
  starting transfers between devices  54.4 us (14%)
  local copies, waits for them, and re-layouts  27.8 us (7%)
  between operations  15.5 us (4%)
    all_to_all x11, blocking collectives, share(): return lax.all_to_all(v, axes, 0, 0)  129 us
    pallas_call x34, Pallas kernels, call(): pl.pallas_call(whole, out_shape=[jax.ShapeDtypeStruct(shape, dtype) for s...  45.4 us
    ppermute x12, waiting for transfers between devices, step(): self.parts = (held, lax.ppermute(held, ALL, exchange(step)))  44.2 us
    ppermute x20, starting transfers between devices, send(): self.terms.append(lax.ppermute(value, ALL, exchange(step)))  21.7 us
    ppermute x20, waiting for transfers between devices, send(): self.terms.append(lax.ppermute(value, ALL, exchange(step)))  21.5 us
    unnamed x183, local copies, waits for them, and re-layouts  20.2 us
    ppermute x12, starting transfers between devices, step(): self.parts = (held, lax.ppermute(held, ALL, exchange(step)))  17.8 us
    ppermute x13, waiting for transfers between devices, over_core(): return lax.ppermute(v, 'core', swap)  8.31 us
  transfers between devices with their start and end apart: 53, of which 27 were waited for; matrix products, arithmetic and copies ran while one was open for 4% of the time, Pallas kernels for 7%

profile of v1, /device:TPU:0, one launch (start us, length us, event | category | flops | bytes accessed | tf_op | source)
XLA Modules:
  0.0 373.0 jit_solution(12279124098524213618)
XLA Ops:
  13.6 2.9 collective-permute-start
  16.7 2.7 collective-permute-start.2
  19.4 4.1 %collective-permute-done.2 = bf16[1,256,128]{2,1,0:T(8,128)(2,1)S(1)} collective-permute-done((bf16[1,256,128]{2,1,0:T(8,128)(2,1)S(1)}, bf16[1,256,128]{2,1,0:T(8,128)(2,1)S(1)}, u32[]{:S(2)}, u32[]{:S(2)}) %collective-permute-start.2) | collective-permute-done | bytes 65568 | tf_op jit(solution)/shard_map/ppermute | solution.py:640
  24.9 4.7 %collective-permute-done.5.refs_2_ = f32[2,4,768]{2,1,0:T(4,128)S(1)} collective-permute-done((f32[2,4,768]{2,1,0:T(4,128)S(1)}, f32[2,4,768]{2,1,0:T(4,128)S(1)}, u32[]{:S(2)}, u32[]{:S(2)}) %collective-permute-start.5) | collective-permute-done | bytes 24608 | tf_op jit(solution)/shard_map/ppermute | solution.py:773
  32.5 3.8 %collective-permute-start.9 = (bf16[1,576,128]{2,1,0:T(8,128)(2,1)}, bf16[1,576,128]{2,1,0:T(8,128)(2,1)S(1)}, u32[]{:S(2)}, u32[]{:S(2)}) collective-permute-start(bf16[1,576,128]{2,1,0:T(8,128)(2,1)} %get-tuple-element.247), channel_id=1, source_target_pairs={{0,4},{1,5},{2,6},{3,7},{4,0},{5,1},{6,2},{7,3},{8,12},{9,13},{10,... | collective-permute-start | bytes 442376 | tf_op jit(solution)/shard_map/ppermute | solution.py:640
  36.4 7.1 %collective-permute-done.9 = bf16[1,576,128]{2,1,0:T(8,128)(2,1)S(1)} collective-permute-done((bf16[1,576,128]{2,1,0:T(8,128)(2,1)}, bf16[1,576,128]{2,1,0:T(8,128)(2,1)S(1)}, u32[]{:S(2)}, u32[]{:S(2)}) %collective-permute-start.9) | collective-permute-done | bytes 147488 | tf_op jit(solution)/shard_map/ppermute | solution.py:640
  46.3 13.4 %collective-permute-done.7.refs_4_.refs_7_ = bf16[8,256,128]{2,1,0:T(8,128)(2,1)S(1)} collective-permute-done((bf16[8,256,128]{2,1,0:T(8,128)(2,1)S(1)}, bf16[8,256,128]{2,1,0:T(8,128)(2,1)S(1)}, u32[]{:S(2)}, u32[]{:S(2)}) %collective-permute-start.7) | collective-permute-done | bytes 524320 | tf_op jit(solution)/shard_map/ppermute | solution.py:640
  64.8 12.1 %all_to_all.65 = f32[32,4,128]{2,1,0:T(4,128)S(1)} all-to-all(f32[32,4,128]{2,1,0:T(4,128)S(1)} %get-tuple-element.240), channel_id=1, replica_groups=mesh['x'=2,'core'=2,'wide'=8] {'x','core','wide'}, dimensions={0} | all-to-all | bytes 131072 | tf_op jit(solution)/shard_map/all_to_all | solution.py:776
  81.6 9.6 %collective-permute-done.14 = bf16[1,256,128]{2,1,0:T(8,128)(2,1)S(1)} collective-permute-done((bf16[1,256,128]{2,1,0:T(8,128)(2,1)S(1)}, bf16[1,256,128]{2,1,0:T(8,128)(2,1)S(1)}, u32[]{:S(2)}, u32[]{:S(2)}) %collective-permute-start.14) | collective-permute-done | bytes 65568 | tf_op jit(solution)/shard_map/ppermute | solution.py:640
  92.3 4.8 %collective-permute-done.15 = bf16[2,256,128]{2,1,0:T(8,128)(2,1)S(1)} collective-permute-done((bf16[2,256,128]{2,1,0:T(8,128)(2,1)S(1)}, bf16[2,256,128]{2,1,0:T(8,128)(2,1)S(1)}, u32[]{:S(2)}, u32[]{:S(2)}) %collective-permute-start.15) | collective-permute-done | bytes 131104 | tf_op jit(solution)/shard_map/ppermute | solution.py:640
  97.1 4.7 %collective-permute-done.12.refs_7_ = bf16[8,576,128]{2,1,0:T(8,128)(2,1)S(1)} collective-permute-done((bf16[8,576,128]{2,1,0:T(8,128)(2,1)S(1)}, bf16[8,576,128]{2,1,0:T(8,128)(2,1)S(1)}, u32[]{:S(2)}, u32[]{:S(2)}) %collective-permute-start.12) | collective-permute-done | bytes 1179680 | tf_op jit(solution)/shard_map/ppermute | solution.py:640
  107.2 2.6 spatial.2
  111.8 2.3 collective-permute-start.17
  114.1 10.8 %all_to_all.66 = f32[32,4,128]{2,1,0:T(4,128)S(1)} all-to-all(f32[32,4,128]{2,1,0:T(4,128)S(1)} %get-tuple-element.253), channel_id=1, replica_groups=mesh['x'=2,'core'=2,'wide'=8] {'x','core','wide'}, dimensions={0} | all-to-all | bytes 131072 | tf_op jit(solution)/shard_map/all_to_all | solution.py:776
  126.5 10.6 %all_to_all.67.refs_0_ = f32[16,16,128]{2,1,0:T(8,128)S(1)} all-to-all(f32[16,16,128]{2,1,0:T(8,128)S(1)} %get-tuple-element.261), channel_id=1, replica_groups=mesh['x'=2,'core'=2,'wide'=8] {'x','wide'}, dimensions={0} | all-to-all | bytes 262144 | tf_op jit(solution)/shard_map/all_to_all | solution.py:776
  138.0 2.5 collective-permute-done.18.refs_2_
  142.0 9.1 %all_to_all.68 = f32[32,4,128]{2,1,0:T(4,128)S(1)} all-to-all(f32[32,4,128]{2,1,0:T(4,128)S(1)} %get-tuple-element.265), channel_id=1, replica_groups=mesh['x'=2,'core'=2,'wide'=8] {'x','core','wide'}, dimensions={0} | all-to-all | bytes 131072 | tf_op jit(solution)/shard_map/all_to_all | solution.py:776
  151.1 2.6 spatial.3
  155.3 9.2 %all_to_all.69 = f32[32,4,128]{2,1,0:T(4,128)S(1)} all-to-all(f32[32,4,128]{2,1,0:T(4,128)S(1)} %get-tuple-element.270), channel_id=1, replica_groups=mesh['x'=2,'core'=2,'wide'=8] {'x','core','wide'}, dimensions={0} | all-to-all | bytes 131072 | tf_op jit(solution)/shard_map/all_to_all | solution.py:776
  165.2 1.7 expand.3
  166.9 11.8 %all_to_all.70.refs_1_ = f32[16,16,128]{2,1,0:T(8,128)S(1)} all-to-all(f32[16,16,128]{2,1,0:T(8,128)S(1)} %get-tuple-element.272), channel_id=1, replica_groups=mesh['x'=2,'core'=2,'wide'=8] {'x','wide'}, dimensions={0} | all-to-all | bytes 262144 | tf_op jit(solution)/shard_map/all_to_all | solution.py:776
  178.7 1.9 last.1
  180.6 10.5 %all_to_all.71.refs_1_ = f32[16,16,128]{2,1,0:T(8,128)S(1)} all-to-all(f32[16,16,128]{2,1,0:T(8,128)S(1)} %get-tuple-element.281), channel_id=1, replica_groups=mesh['x'=2,'core'=2,'wide'=8] {'x','wide'}, dimensions={0} | all-to-all | bytes 262144 | tf_op jit(solution)/shard_map/all_to_all | solution.py:776
  191.1 1.8 expand_back.2
  197.0 9.4 %all_to_all.72 = f32[32,4,128]{2,1,0:T(4,128)S(1)} all-to-all(f32[32,4,128]{2,1,0:T(4,128)S(1)} %get-tuple-element.291), channel_id=1, replica_groups=mesh['x'=2,'core'=2,'wide'=8] {'x','core','wide'}, dimensions={0} | all-to-all | bytes 131072 | tf_op jit(solution)/shard_map/all_to_all | solution.py:776
  206.4 2.4 spatial_back.2
  208.8 2.1 spatial_grad.2
  213.6 14.6 %all_to_all.73 = f32[32,4,128]{2,1,0:T(4,128)S(1)} all-to-all(f32[32,4,128]{2,1,0:T(4,128)S(1)} %get-tuple-element.302), channel_id=1, replica_groups=mesh['x'=2,'core'=2,'wide'=8] {'x','core','wide'}, dimensions={0} | all-to-all | bytes 131072 | tf_op jit(solution)/shard_map/all_to_all | solution.py:776
  234.2 21.5 %all_to_all.74.refs_1_ = f32[16,16,128]{2,1,0:T(8,128)S(1)} all-to-all(f32[16,16,128]{2,1,0:T(8,128)S(1)} %get-tuple-element.315), channel_id=1, replica_groups=mesh['x'=2,'core'=2,'wide'=8] {'x','wide'}, dimensions={0} | all-to-all | bytes 262144 | tf_op jit(solution)/shard_map/all_to_all | solution.py:776
  263.3 9.5 %all_to_all.75 = f32[32,4,128]{2,1,0:T(4,128)S(1)} all-to-all(f32[32,4,128]{2,1,0:T(4,128)S(1)} %get-tuple-element.331), channel_id=1, replica_groups=mesh['x'=2,'core'=2,'wide'=8] {'x','core','wide'}, dimensions={0} | all-to-all | bytes 131072 | tf_op jit(solution)/shard_map/all_to_all | solution.py:776
  274.2 2.0 spatial_back.3
  276.1 3.2 spatial_grad.3
  285.3 3.4 all-to-all-start.11
  288.7 7.3 %collective-permute-done.33.refs_6_ = bf16[1,832,128]{2,1,0:T(8,128)(2,1)} collective-permute-done((bf16[1,832,128]{2,1,0:T(8,128)(2,1)}, bf16[1,832,128]{2,1,0:T(8,128)(2,1)}, u32[]{:S(2)}, u32[]{:S(2)}) %collective-permute-start.33) | collective-permute-done | bytes 213024 | tf_op jit(solution)/shard_map/ppermute | solution.py:681
  296.4 6.0 %all-to-all-done.11 = f32[32,4,128]{2,1,0:T(4,128)} async-done(((f32[32,4,128]{2,1,0:T(4,128)}), f32[32,4,128]{2,1,0:T(4,128)}, u32[]{:S(2)}, u32[]{:S(2)}) %all-to-all-start.11) | async-done | bytes 65568 | tf_op jit(solution)/shard_map/all_to_all | solution.py:776
  304.5 1.7 reduce_back.3
  312.0 1.7 collective-permute-start.42
  314.4 3.7 collective-permute-done.41.refs_5_.refs_3_
  318.1 1.7 collective-permute-done.42.refs_9_.refs_7_
  323.7 1.7 collective-permute-start.37
  327.5 1.9 collective-permute-start.46
  329.5 2.5 lamb.3
  334.2 3.4 collective-permute-done.46.refs_8_
  337.6 1.9 collective-permute-done.44.refs_3_
  344.6 2.0 lamb.4
  353.0 3.8 %all-to-all-start.12 = ((f32[32,1,128]{2,1,0:T(1,128)}), f32[32,1,128]{2,1,0:T(1,128)S(1)}, u32[]{:S(2)}, u32[]{:S(2)}) async-start(f32[32,1,128]{2,1,0:T(1,128)} %get-tuple-element.447), calls=%async_computation.12 | async-start | bytes 32768 | tf_op jit(solution)/shard_map/all_to_all | solution.py:776
  356.8 3.8 %copy.49 = f32[4,14,14,512]{3,0,2,1:T(4,128)} copy(f32[4,14,14,512]{3,2,1,0:T(8,128)} %copy-done.23) | data formatting | bytes 3211264
  360.6 2.2 copy.50
  (331 shorter events, 96.9 us)
Async XLA Ops:
  7.2 99.0 %all-gather.3.cloned.1.call-start = ((), (), s32[]{:S(2)}) async-start(), calls=%async_computation.13 | async-start | bytes 4734976 | tf_op jit(solution)/shard_map/all_gather | solution.py:820
  13.6 16.5 %collective-permute-start = (bf16[448,512]{1,0:T(8,128)(2,1)S(1)}, bf16[448,512]{1,0:T(8,128)(2,1)S(1)}, u32[]{:S(2)}, u32[]{:S(2)}) collective-permute-start(bf16[448,512]{1,0:T(8,128)(2,1)S(1)} %get-tuple-element.236), channel_id=1, source_target_pairs={{0,16},{16,0},{1,17},{17,1},{2,18},{18,2},{3,19},{19,3},{4,20},{20... | collective-permute-start | bytes 1376264 | tf_op jit(solution)/shard_map/ppermute | solution.py:773
  16.6 7.7 %collective-permute-start.4 = (f32[4,768]{1,0:T(4,128)S(1)}, f32[4,768]{1,0:T(4,128)S(1)}, u32[]{:S(2)}, u32[]{:S(2)}) collective-permute-start(f32[4,768]{1,0:T(4,128)S(1)} %reshape.68), channel_id=1, source_target_pairs={{0,8},{8,0},{1,9},{9,1},{2,10},{10,2},{3,11},{11,3},{4,12},{12,4},... | collective-permute-start | bytes 36872 | tf_op jit(solution)/shard_map/ppermute | solution.py:770
  16.7 6.8 %collective-permute-start.2 = (bf16[1,256,128]{2,1,0:T(8,128)(2,1)S(1)}, bf16[1,256,128]{2,1,0:T(8,128)(2,1)S(1)}, u32[]{:S(2)}, u32[]{:S(2)}) collective-permute-start(bf16[1,256,128]{2,1,0:T(8,128)(2,1)S(1)} %get-tuple-element.237), channel_id=1, source_target_pairs={{0,4},{1,5},{2,6},{3,7},{4,0},{5,1},{6,2},{7,3},{8,12},{9,13},{10,... | collective-permute-start | bytes 196616 | tf_op jit(solution)/shard_map/ppermute | solution.py:640
  23.6 6.6 %collective-permute-start.3 = (bf16[2,256,128]{2,1,0:T(8,128)(2,1)S(1)}, bf16[2,256,128]{2,1,0:T(8,128)(2,1)S(1)}, u32[]{:S(2)}, u32[]{:S(2)}) collective-permute-start(bf16[2,256,128]{2,1,0:T(8,128)(2,1)S(1)} %constant_dynamic-update-slice_fusion), channel_id=1, source_target_pairs={{0,2},{1,3},{2,0},{3,1},{4,6},{5,7},{6,4},{7,5},{8,10},{9,11},{10,... | collective-permute-start | bytes 393224 | tf_op jit(solution)/shard_map/ppermute | solution.py:640
  24.3 5.3 %collective-permute-start.5 = (f32[2,4,768]{2,1,0:T(4,128)S(1)}, f32[2,4,768]{2,1,0:T(4,128)S(1)}, u32[]{:S(2)}, u32[]{:S(2)}) collective-permute-start(f32[2,4,768]{2,1,0:T(4,128)S(1)} %pad_maximum_fusion.1.refs_1_), channel_id=1, source_target_pairs={{0,16},{16,0},{1,17},{17,1},{2,18},{18,2},{3,19},{19,3},{4,20},{20... | collective-permute-start | bytes 73736 | tf_op jit(solution)/shard_map/ppermute | solution.py:773
  30.8 28.9 %collective-permute-start.1 = (bf16[448,1024]{1,0:T(8,128)(2,1)S(1)}, bf16[448,1024]{1,0:T(8,128)(2,1)S(1)}, u32[]{:S(2)}, u32[]{:S(2)}) collective-permute-start(bf16[448,1024]{1,0:T(8,128)(2,1)S(1)} %join.1.refs_1_.refs_2_), channel_id=1, source_target_pairs={{0,8},{8,0},{1,9},{9,1},{2,10},{10,2},{3,11},{11,3},{4,12},{12,4},... | collective-permute-start | bytes 2752520 | tf_op jit(solution)/shard_map/ppermute | solution.py:770
  30.9 12.5 %collective-permute-start.6 = (bf16[4,256,128]{2,1,0:T(8,128)(2,1)S(1)}, bf16[4,256,128]{2,1,0:T(8,128)(2,1)S(1)}, u32[]{:S(2)}, u32[]{:S(2)}) collective-permute-start(bf16[4,256,128]{2,1,0:T(8,128)(2,1)S(1)} %get-tuple-element.491), channel_id=1, source_target_pairs={{0,1},{1,0},{2,3},{3,2},{4,5},{5,4},{6,7},{7,6},{8,24},{9,25},{10,... | collective-permute-start | bytes 786440 | tf_op jit(solution)/shard_map/ppermute | solution.py:640
  32.5 10.9 %collective-permute-start.9 = (bf16[1,576,128]{2,1,0:T(8,128)(2,1)}, bf16[1,576,128]{2,1,0:T(8,128)(2,1)S(1)}, u32[]{:S(2)}, u32[]{:S(2)}) collective-permute-start(bf16[1,576,128]{2,1,0:T(8,128)(2,1)} %get-tuple-element.247), channel_id=1, source_target_pairs={{0,4},{1,5},{2,6},{3,7},{4,0},{5,1},{6,2},{7,3},{8,12},{9,13},{10,... | collective-permute-start | bytes 442376 | tf_op jit(solution)/shard_map/ppermute | solution.py:640
  43.5 16.2 %collective-permute-start.7 = (bf16[8,256,128]{2,1,0:T(8,128)(2,1)S(1)}, bf16[8,256,128]{2,1,0:T(8,128)(2,1)S(1)}, u32[]{:S(2)}, u32[]{:S(2)}) collective-permute-start(bf16[8,256,128]{2,1,0:T(8,128)(2,1)S(1)} %constant_dynamic-update-slice_fusion.4.refs_3_.refs_6_), channel_id=1, source_target_pairs={{0,16},{1,17},{2,18},{3,19},{4,20},{5,21},{6,22},{7,23},{8,9},{9,8... | collective-permute-start | bytes 1572872 | tf_op jit(solution)/shard_map/ppermute | solution.py:640
  46.2 14.9 %collective-permute-start.10 = (bf16[2,576,128]{2,1,0:T(8,128)(2,1)}, bf16[2,576,128]{2,1,0:T(8,128)(2,1)}, u32[]{:S(2)}, u32[]{:S(2)}) collective-permute-start(bf16[2,576,128]{2,1,0:T(8,128)(2,1)} %constant_dynamic-update-slice_fusion.7), channel_id=1, source_target_pairs={{0,2},{1,3},{2,0},{3,1},{4,6},{5,7},{6,4},{7,5},{8,10},{9,11},{10,... | collective-permute-start | bytes 884744 | tf_op jit(solution)/shard_map/ppermute | solution.py:640
  63.3 13.6 %collective-permute-start.11 = (bf16[4,576,128]{2,1,0:T(8,128)(2,1)S(1)}, bf16[4,576,128]{2,1,0:T(8,128)(2,1)S(1)}, u32[]{:S(2)}, u32[]{:S(2)}) collective-permute-start(bf16[4,576,128]{2,1,0:T(8,128)(2,1)S(1)} %constant_dynamic-update-slice_fusion.9), channel_id=1, source_target_pairs={{0,1},{1,0},{2,3},{3,2},{4,5},{5,4},{6,7},{7,6},{8,24},{9,25},{10,... | collective-permute-start | bytes 1769480 | tf_op jit(solution)/shard_map/ppermute | solution.py:640
  77.0 24.7 %collective-permute-start.12 = (bf16[8,576,128]{2,1,0:T(8,128)(2,1)S(1)}, bf16[8,576,128]{2,1,0:T(8,128)(2,1)S(1)}, u32[]{:S(2)}, u32[]{:S(2)}) collective-permute-start(bf16[8,576,128]{2,1,0:T(8,128)(2,1)S(1)} %constant_dynamic-update-slice_fusion.11.refs_6_), channel_id=1, source_target_pairs={{0,16},{1,17},{2,18},{3,19},{4,20},{5,21},{6,22},{7,23},{8,9},{9,8... | collective-permute-start | bytes 3538952 | tf_op jit(solution)/shard_map/ppermute | solution.py:640
  80.5 10.7 %collective-permute-start.14 = (bf16[1,256,128]{2,1,0:T(8,128)(2,1)S(1)}, bf16[1,256,128]{2,1,0:T(8,128)(2,1)S(1)}, u32[]{:S(2)}, u32[]{:S(2)}) collective-permute-start(bf16[1,256,128]{2,1,0:T(8,128)(2,1)S(1)} %bitcast.37), channel_id=1, source_target_pairs={{0,4},{1,5},{2,6},{3,7},{4,0},{5,1},{6,2},{7,3},{8,12},{9,13},{10,... | collective-permute-start | bytes 196616 | tf_op jit(solution)/shard_map/ppermute | solution.py:640
  91.2 5.8 %collective-permute-start.15 = (bf16[2,256,128]{2,1,0:T(8,128)(2,1)S(1)}, bf16[2,256,128]{2,1,0:T(8,128)(2,1)S(1)}, u32[]{:S(2)}, u32[]{:S(2)}) collective-permute-start(bf16[2,256,128]{2,1,0:T(8,128)(2,1)S(1)} %constant_dynamic-update-slice_fusion.13), channel_id=1, source_target_pairs={{0,2},{1,3},{2,0},{3,1},{4,6},{5,7},{6,4},{7,5},{8,10},{9,11},{10,... | collective-permute-start | bytes 393224 | tf_op jit(solution)/shard_map/ppermute | solution.py:640
  91.9 14.3 %collective-permute-start.8 = (bf16[448,256]{1,0:T(8,128)(2,1)}, bf16[448,256]{1,0:T(8,128)(2,1)}, u32[]{:S(2)}, u32[]{:S(2)}) collective-permute-start(bf16[448,256]{1,0:T(8,128)(2,1)} %copy-done.81), channel_id=1, source_target_pairs={{0,8},{8,0},{1,9},{9,1},{2,10},{10,2},{3,11},{11,3},{4,12},{12,4},... | collective-permute-start | bytes 688136 | tf_op jit(solution)/shard_map/ppermute | solution.py:770
  103.1 6.7 %collective-permute-start.16 = (bf16[4,256,128]{2,1,0:T(8,128)(2,1)}, bf16[4,256,128]{2,1,0:T(8,128)(2,1)}, u32[]{:S(2)}, u32[]{:S(2)}) collective-permute-start(bf16[4,256,128]{2,1,0:T(8,128)(2,1)} %constant_dynamic-update-slice_fusion.15), channel_id=1, source_target_pairs={{0,1},{1,0},{2,3},{3,2},{4,5},{5,4},{6,7},{7,6},{8,24},{9,25},{10,... | collective-permute-start | bytes 786440 | tf_op jit(solution)/shard_map/ppermute | solution.py:640
  111.8 13.1 %collective-permute-start.17 = (bf16[8,256,128]{2,1,0:T(8,128)(2,1)S(1)}, bf16[8,256,128]{2,1,0:T(8,128)(2,1)S(1)}, u32[]{:S(2)}, u32[]{:S(2)}) collective-permute-start(bf16[8,256,128]{2,1,0:T(8,128)(2,1)S(1)} %constant_dynamic-update-slice_fusion.17.refs_6_), channel_id=1, source_target_pairs={{0,16},{1,17},{2,18},{3,19},{4,20},{5,21},{6,22},{7,23},{8,9},{9,8... | collective-permute-start | bytes 1572872 | tf_op jit(solution)/shard_map/ppermute | solution.py:640
  114.1 10.8 %collective-permute-start.13 = (bf16[448,256]{1,0:T(8,128)(2,1)S(1)}, bf16[448,256]{1,0:T(8,128)(2,1)S(1)}, u32[]{:S(2)}, u32[]{:S(2)}) collective-permute-start(bf16[448,256]{1,0:T(8,128)(2,1)S(1)} %get-tuple-element.255), channel_id=1, source_target_pairs={{0,8},{8,0},{1,9},{9,1},{2,10},{10,2},{3,11},{11,3},{4,12},{12,4},... | collective-permute-start | bytes 688136 | tf_op jit(solution)/shard_map/ppermute | solution.py:770
  141.8 9.3 %collective-permute-start.19 = (bf16[448,256]{1,0:T(8,128)(2,1)S(1)}, bf16[448,256]{1,0:T(8,128)(2,1)S(1)}, u32[]{:S(2)}, u32[]{:S(2)}) collective-permute-start(bf16[448,256]{1,0:T(8,128)(2,1)S(1)} %get-tuple-element.267), channel_id=1, source_target_pairs={{0,8},{8,0},{1,9},{9,1},{2,10},{10,2},{3,11},{11,3},{4,12},{12,4},... | collective-permute-start | bytes 688136 | tf_op jit(solution)/shard_map/ppermute | solution.py:770
  164.5 14.2 %collective-permute-start.21 = (bf16[448,512]{1,0:T(8,128)(2,1)S(1)}, bf16[448,512]{1,0:T(8,128)(2,1)S(1)}, u32[]{:S(2)}, u32[]{:S(2)}) collective-permute-start(bf16[448,512]{1,0:T(8,128)(2,1)S(1)} %copy-done.80), channel_id=1, source_target_pairs={{0,16},{16,0},{1,17},{17,1},{2,18},{18,2},{3,19},{19,3},{4,20},{20... | collective-permute-start | bytes 1376264 | tf_op jit(solution)/shard_map/ppermute | solution.py:773
  194.3 12.2 %collective-permute-start.23 = (bf16[8,256,128]{2,1,0:T(8,128)(2,1)S(1)}, bf16[8,256,128]{2,1,0:T(8,128)(2,1)S(1)}, u32[]{:S(2)}, u32[]{:S(2)}) collective-permute-start(bf16[8,256,128]{2,1,0:T(8,128)(2,1)S(1)} %get-tuple-element.287), channel_id=1, source_target_pairs={{0,16},{1,17},{2,18},{3,19},{4,20},{5,21},{6,22},{7,23},{8,9},{9,8... | collective-permute-start | bytes 1572872 | tf_op jit(solution)/shard_map/ppermute | solution.py:681
  211.0 17.1 %collective-permute-start.25 = (bf16[8,576,128]{2,1,0:T(8,128)(2,1)S(1)}, bf16[8,576,128]{2,1,0:T(8,128)(2,1)S(1)}, u32[]{:S(2)}, u32[]{:S(2)}) collective-permute-start(bf16[8,576,128]{2,1,0:T(8,128)(2,1)S(1)} %get-tuple-element.298), channel_id=1, source_target_pairs={{0,16},{1,17},{2,18},{3,19},{4,20},{5,21},{6,22},{7,23},{8,9},{9,8... | collective-permute-start | bytes 3538952 | tf_op jit(solution)/shard_map/ppermute | solution.py:681
  229.8 2.9 collective-permute-start.26
  230.0 25.7 %collective-permute-start.27 = (bf16[4,832,128]{2,1,0:T(8,128)(2,1)S(1)}, bf16[4,832,128]{2,1,0:T(8,128)(2,1)S(1)}, u32[]{:S(2)}, u32[]{:S(2)}) collective-permute-start(bf16[4,832,128]{2,1,0:T(8,128)(2,1)S(1)} %add_up.10), channel_id=1, source_target_pairs={{0,1},{1,0},{2,3},{3,2},{4,5},{5,4},{6,7},{7,6},{8,24},{9,25},{10,... | collective-permute-start | bytes 2555912 | tf_op jit(solution)/shard_map/ppermute | solution.py:681
  255.8 17.0 %collective-permute-start.30 = (bf16[8,256,128]{2,1,0:T(8,128)(2,1)S(1)}, bf16[8,256,128]{2,1,0:T(8,128)(2,1)S(1)}, u32[]{:S(2)}, u32[]{:S(2)}) collective-permute-start(bf16[8,256,128]{2,1,0:T(8,128)(2,1)S(1)} %get-tuple-element.334), channel_id=1, source_target_pairs={{0,16},{1,17},{2,18},{3,19},{4,20},{5,21},{6,22},{7,23},{8,9},{9,8... | collective-permute-start | bytes 1572872 | tf_op jit(solution)/shard_map/ppermute | solution.py:681
  259.5 13.3 %collective-permute-start.29 = (bf16[8,256,128]{2,1,0:T(8,128)(2,1)S(1)}, bf16[8,256,128]{2,1,0:T(8,128)(2,1)S(1)}, u32[]{:S(2)}, u32[]{:S(2)}) collective-permute-start(bf16[8,256,128]{2,1,0:T(8,128)(2,1)S(1)} %get-tuple-element.327), channel_id=1, source_target_pairs={{0,16},{1,17},{2,18},{3,19},{4,20},{5,21},{6,22},{7,23},{8,9},{9,8... | collective-permute-start | bytes 1572872 | tf_op jit(solution)/shard_map/ppermute | solution.py:681
  260.8 12.0 %collective-permute-start.31 = (bf16[2,832,128]{2,1,0:T(8,128)(2,1)S(1)}, bf16[2,832,128]{2,1,0:T(8,128)(2,1)S(1)}, u32[]{:S(2)}, u32[]{:S(2)}) collective-permute-start(bf16[2,832,128]{2,1,0:T(8,128)(2,1)S(1)} %add_up.11), channel_id=1, source_target_pairs={{0,2},{1,3},{2,0},{3,1},{4,6},{5,7},{6,4},{7,5},{8,10},{9,11},{10,... | collective-permute-start | bytes 1277960 | tf_op jit(solution)/shard_map/ppermute | solution.py:681
  279.3 23.1 %collective-permute-start.36 = (bf16[8,576,128]{2,1,0:T(8,128)(2,1)}, bf16[8,576,128]{2,1,0:T(8,128)(2,1)S(1)}, u32[]{:S(2)}, u32[]{:S(2)}) collective-permute-start(bf16[8,576,128]{2,1,0:T(8,128)(2,1)} %get-tuple-element.352), channel_id=1, source_target_pairs={{0,16},{1,17},{2,18},{3,19},{4,20},{5,21},{6,22},{7,23},{8,9},{9,8... | collective-permute-start | bytes 3538952 | tf_op jit(solution)/shard_map/ppermute | solution.py:681
  280.8 2.8 collective-permute-start.32
  280.8 15.2 %collective-permute-start.34 = (bf16[4,256,128]{2,1,0:T(8,128)(2,1)}, bf16[4,256,128]{2,1,0:T(8,128)(2,1)S(1)}, u32[]{:S(2)}, u32[]{:S(2)}) collective-permute-start(bf16[4,256,128]{2,1,0:T(8,128)(2,1)} %get-tuple-element.343), channel_id=1, source_target_pairs={{0,1},{1,0},{2,3},{3,2},{4,5},{5,4},{6,7},{7,6},{8,24},{9,25},{10,... | collective-permute-start | bytes 786440 | tf_op jit(solution)/shard_map/ppermute | solution.py:681
  281.5 14.9 %collective-permute-start.35 = (bf16[4,256,128]{2,1,0:T(8,128)(2,1)}, bf16[4,256,128]{2,1,0:T(8,128)(2,1)}, u32[]{:S(2)}, u32[]{:S(2)}) collective-permute-start(bf16[4,256,128]{2,1,0:T(8,128)(2,1)} %get-tuple-element.344), channel_id=1, source_target_pairs={{0,1},{1,0},{2,3},{3,2},{4,5},{5,4},{6,7},{7,6},{8,24},{9,25},{10,... | collective-permute-start | bytes 786440 | tf_op jit(solution)/shard_map/ppermute | solution.py:681
  282.8 13.2 %collective-permute-start.33 = (bf16[1,832,128]{2,1,0:T(8,128)(2,1)}, bf16[1,832,128]{2,1,0:T(8,128)(2,1)}, u32[]{:S(2)}, u32[]{:S(2)}) collective-permute-start(bf16[1,832,128]{2,1,0:T(8,128)(2,1)} %get-tuple-element.345), channel_id=1, source_target_pairs={{0,4},{1,5},{2,6},{3,7},{4,0},{5,1},{6,2},{7,3},{8,12},{9,13},{10,... | collective-permute-start | bytes 638984 | tf_op jit(solution)/shard_map/ppermute | solution.py:681
  285.3 17.1 %all-to-all-start.11 = ((f32[32,4,128]{2,1,0:T(4,128)}), f32[32,4,128]{2,1,0:T(4,128)}, u32[]{:S(2)}, u32[]{:S(2)}) async-start(f32[32,4,128]{2,1,0:T(4,128)} %copy-done.62), calls=%async_computation.11 | async-start | bytes 131072 | tf_op jit(solution)/shard_map/all_to_all | solution.py:776
  306.3 19.2 %collective-permute-start.38 = (bf16[448,1024]{1,0:T(8,128)(2,1)S(1)}, bf16[448,1024]{1,0:T(8,128)(2,1)S(1)}, u32[]{:S(2)}, u32[]{:S(2)}) collective-permute-start(bf16[448,1024]{1,0:T(8,128)(2,1)S(1)} %get-tuple-element.370), channel_id=1, source_target_pairs={{0,8},{8,0},{1,9},{9,1},{2,10},{10,2},{3,11},{11,3},{4,12},{12,4},... | collective-permute-start | bytes 2752520 | tf_op jit(solution)/shard_map/ppermute | solution.py:770
  306.4 14.1 %collective-permute-start.40 = (bf16[4,576,128]{2,1,0:T(8,128)(2,1)S(1)}, bf16[4,576,128]{2,1,0:T(8,128)(2,1)S(1)}, u32[]{:S(2)}, u32[]{:S(2)}) collective-permute-start(bf16[4,576,128]{2,1,0:T(8,128)(2,1)S(1)} %add_up.13), channel_id=1, source_target_pairs={{0,1},{1,0},{2,3},{3,2},{4,5},{5,4},{6,7},{7,6},{8,24},{9,25},{10,... | collective-permute-start | bytes 1769480 | tf_op jit(solution)/shard_map/ppermute | solution.py:681
  309.1 12.3 %collective-permute-start.39 = (bf16[8,256,128]{2,1,0:T(8,128)(2,1)S(1)}, bf16[8,256,128]{2,1,0:T(8,128)(2,1)S(1)}, u32[]{:S(2)}, u32[]{:S(2)}) collective-permute-start(bf16[8,256,128]{2,1,0:T(8,128)(2,1)S(1)} %get-tuple-element.368), channel_id=1, source_target_pairs={{0,16},{1,17},{2,18},{3,19},{4,20},{5,21},{6,22},{7,23},{8,9},{9,8... | collective-permute-start | bytes 1572872 | tf_op jit(solution)/shard_map/ppermute | solution.py:681
  311.6 6.4 %collective-permute-start.41 = (bf16[2,256,128]{2,1,0:T(8,128)(2,1)S(1)}, bf16[2,256,128]{2,1,0:T(8,128)(2,1)S(1)}, u32[]{:S(2)}, u32[]{:S(2)}) collective-permute-start(bf16[2,256,128]{2,1,0:T(8,128)(2,1)S(1)} %get-tuple-element.377), channel_id=1, source_target_pairs={{0,2},{1,3},{2,0},{3,1},{4,6},{5,7},{6,4},{7,5},{8,10},{9,11},{10,... | collective-permute-start | bytes 393224 | tf_op jit(solution)/shard_map/ppermute | solution.py:681
  312.0 7.8 %collective-permute-start.42 = (bf16[2,256,128]{2,1,0:T(8,128)(2,1)S(1)}, bf16[2,256,128]{2,1,0:T(8,128)(2,1)S(1)}, u32[]{:S(2)}, u32[]{:S(2)}) collective-permute-start(bf16[2,256,128]{2,1,0:T(8,128)(2,1)S(1)} %get-tuple-element.378), channel_id=1, source_target_pairs={{0,2},{1,3},{2,0},{3,1},{4,6},{5,7},{6,4},{7,5},{8,10},{9,11},{10,... | collective-permute-start | bytes 393224 | tf_op jit(solution)/shard_map/ppermute | solution.py:681
  322.5 10.8 %collective-permute-start.45 = (bf16[4,256,128]{2,1,0:T(8,128)(2,1)S(1)}, bf16[4,256,128]{2,1,0:T(8,128)(2,1)S(1)}, u32[]{:S(2)}, u32[]{:S(2)}) collective-permute-start(bf16[4,256,128]{2,1,0:T(8,128)(2,1)S(1)} %get-tuple-element.392), channel_id=1, source_target_pairs={{0,1},{1,0},{2,3},{3,2},{4,5},{5,4},{6,7},{7,6},{8,24},{9,25},{10,... | collective-permute-start | bytes 786440 | tf_op jit(solution)/shard_map/ppermute | solution.py:681
  323.7 18.9 %collective-permute-start.37 = (bf16[448,512]{1,0:T(8,128)(2,1)S(1)}, bf16[448,512]{1,0:T(8,128)(2,1)S(1)}, u32[]{:S(2)}, u32[]{:S(2)}) collective-permute-start(bf16[448,512]{1,0:T(8,128)(2,1)S(1)} %get-tuple-element.366), channel_id=1, source_target_pairs={{0,16},{16,0},{1,17},{17,1},{2,18},{18,2},{3,19},{19,3},{4,20},{20... | collective-permute-start | bytes 1376264 | tf_op jit(solution)/shard_map/ppermute | solution.py:773
  326.3 20.7 %collective-permute-start.43 = (bf16[448,512]{1,0:T(8,128)(2,1)S(1)}, bf16[448,512]{1,0:T(8,128)(2,1)S(1)}, u32[]{:S(2)}, u32[]{:S(2)}) collective-permute-start(bf16[448,512]{1,0:T(8,128)(2,1)S(1)} %get-tuple-element.397), channel_id=1, source_target_pairs={{0,16},{16,0},{1,17},{17,1},{2,18},{18,2},{3,19},{19,3},{4,20},{20... | collective-permute-start | bytes 1376264 | tf_op jit(solution)/shard_map/ppermute | solution.py:773
  326.8 12.7 %collective-permute-start.44 = (bf16[2,576,128]{2,1,0:T(8,128)(2,1)S(1)}, bf16[2,576,128]{2,1,0:T(8,128)(2,1)S(1)}, u32[]{:S(2)}, u32[]{:S(2)}) collective-permute-start(bf16[2,576,128]{2,1,0:T(8,128)(2,1)S(1)} %add_up.15), channel_id=1, source_target_pairs={{0,2},{1,3},{2,0},{3,1},{4,6},{5,7},{6,4},{7,5},{8,10},{9,11},{10,... | collective-permute-start | bytes 884744 | tf_op jit(solution)/shard_map/ppermute | solution.py:681
  327.5 10.1 %collective-permute-start.46 = (bf16[1,512,128]{2,1,0:T(8,128)(2,1)S(1)}, bf16[1,512,128]{2,1,0:T(8,128)(2,1)S(1)}, u32[]{:S(2)}, u32[]{:S(2)}) collective-permute-start(bf16[1,512,128]{2,1,0:T(8,128)(2,1)S(1)} %get-tuple-element.398), channel_id=1, source_target_pairs={{0,4},{1,5},{2,6},{3,7},{4,0},{5,1},{6,2},{7,3},{8,12},{9,13},{10,... | collective-permute-start | bytes 393224 | tf_op jit(solution)/shard_map/ppermute | solution.py:681
  333.4 8.6 %collective-permute-start.48 = (bf16[2,256,128]{2,1,0:T(8,128)(2,1)S(1)}, bf16[2,256,128]{2,1,0:T(8,128)(2,1)S(1)}, u32[]{:S(2)}, u32[]{:S(2)}) collective-permute-start(bf16[2,256,128]{2,1,0:T(8,128)(2,1)S(1)} %add_up.17), channel_id=1, source_target_pairs={{0,2},{1,3},{2,0},{3,1},{4,6},{5,7},{6,4},{7,5},{8,10},{9,11},{10,... | collective-permute-start | bytes 393224 | tf_op jit(solution)/shard_map/ppermute | solution.py:681
  339.6 10.3 %collective-permute-start.47 = (bf16[1,576,128]{2,1,0:T(8,128)(2,1)S(1)}, bf16[1,576,128]{2,1,0:T(8,128)(2,1)S(1)}, u32[]{:S(2)}, u32[]{:S(2)}) collective-permute-start(bf16[1,576,128]{2,1,0:T(8,128)(2,1)S(1)} %add_up.18), channel_id=1, source_target_pairs={{0,4},{1,5},{2,6},{3,7},{4,0},{5,1},{6,2},{7,3},{8,12},{9,13},{10,... | collective-permute-start | bytes 442376 | tf_op jit(solution)/shard_map/ppermute | solution.py:681
  342.0 7.9 %collective-permute-start.49 = (bf16[1,256,128]{2,1,0:T(8,128)(2,1)S(1)}, bf16[1,256,128]{2,1,0:T(8,128)(2,1)S(1)}, u32[]{:S(2)}, u32[]{:S(2)}) collective-permute-start(bf16[1,256,128]{2,1,0:T(8,128)(2,1)S(1)} %add_up.19), channel_id=1, source_target_pairs={{0,4},{1,5},{2,6},{3,7},{4,0},{5,1},{6,2},{7,3},{8,12},{9,13},{10,... | collective-permute-start | bytes 196616 | tf_op jit(solution)/shard_map/ppermute | solution.py:681
  353.0 10.9 %all-to-all-start.12 = ((f32[32,1,128]{2,1,0:T(1,128)}), f32[32,1,128]{2,1,0:T(1,128)S(1)}, u32[]{:S(2)}, u32[]{:S(2)}) async-start(f32[32,1,128]{2,1,0:T(1,128)} %get-tuple-element.447), calls=%async_computation.12 | async-start | bytes 32768 | tf_op jit(solution)/shard_map/all_to_all | solution.py:776
  (90 other events, 1203.8 us)
Sparse Core Ops, SparseCore 0:
  11.7 94.4 all-gather.2

commit v2 on v1

--- a/solution.py
+++ b/solution.py
@@ -1060,6 +1060,8 @@
         recv = over_core(send)
         grad_spatial = gradient(b, 1, spatial_grad, item["hid1"], shifts, name="spatial_grad")
         own_part = order(own_part, *grad_spatial, *hook("spatial", b, grad_spatial))
+        if fast and b == 0:
+            own_part = order(own_part, *(tasks[name].terms[-1] for name in ("big", ("expand", 0), ("reduce", 1))))
         upstream, stat = call(
             functools.partial(inner_back_kernel, 0),
             [((ROWS, 256), F32), (inner, F32)],

time: 376 us -> 376 us (level)
  blocking collectives: 129 us -> 146 us
  starting transfers between devices: 54.4 us -> 42.2 us
  waiting for transfers between devices: 87.7 us -> 95.3 us
  local copies, waits for them, and re-layouts: 27.8 us -> 20.6 us
  Pallas kernels: 55.7 us -> 51.4 us
    all_to_all x11 -> x12, blocking collectives: 129 us -> 146 us  [share(): return lax.all_to_all(v, axes, 0, 0)]
    ppermute x20, waiting for transfers between devices: 21.5 us -> 30.2 us  [send(): self.terms.append(lax.ppermute(value, ALL, exchange(step)))]
    unnamed x183 -> x85, local copies, waits for them, and re-layouts: 20.2 us -> 14.7 us
    ppermute x12, starting transfers between devices: 17.8 us -> 12.6 us  [step(): self.parts = (held, lax.ppermute(held, ALL, exchange(step)))]
    all_to_all x2 -> x1, starting transfers between devices: 7.16 us -> 2.68 us  [share(): return lax.all_to_all(v, axes, 0, 0)]
    all_to_all x2 -> x1, waiting for transfers between devices: 7.02 us -> 2.62 us  [share(): return lax.all_to_all(v, axes, 0, 0)]
  transfers between devices with their start and end apart: 53 -> 52, of which waited for: 27 -> 25; matrix products, arithmetic and copies ran while one was open for 4% -> 3% of each run, Pallas kernels for 7% -> 7%
where the time goes in v2:
time: 376 us; the launch traced here: 373 us
  blocking collectives  146 us (39%)
  waiting for transfers between devices  95.3 us (25%)
  Pallas kernels  51.4 us (14%)
  starting transfers between devices  42.2 us (11%)
  local copies, waits for them, and re-layouts  20.6 us (5%)
  between operations  15 us (4%)
    all_to_all x12, blocking collectives, share(): return lax.all_to_all(v, axes, 0, 0)  146 us
    ppermute x12, waiting for transfers between devices, step(): self.parts = (held, lax.ppermute(held, ALL, exchange(step)))  47.1 us
    pallas_call x34, Pallas kernels, call(): pl.pallas_call(whole, out_shape=[jax.ShapeDtypeStruct(shape, dtype) for s...  45.8 us
    ppermute x20, waiting for transfers between devices, send(): self.terms.append(lax.ppermute(value, ALL, exchange(step)))  30.2 us
    ppermute x20, starting transfers between devices, send(): self.terms.append(lax.ppermute(value, ALL, exchange(step)))  19.6 us
    unnamed x85, local copies, waits for them, and re-layouts  14.7 us
    ppermute x12, starting transfers between devices, step(): self.parts = (held, lax.ppermute(held, ALL, exchange(step)))  12.6 us
    ppermute x13, waiting for transfers between devices, over_core(): return lax.ppermute(v, 'core', swap)  8.31 us
  transfers between devices with their start and end apart: 52, of which 25 were waited for; matrix products, arithmetic and copies ran while one was open for 3% of the time, Pallas kernels for 7%

profile of v2, /device:TPU:0, one launch (start us, length us, event | category | flops | bytes accessed | tf_op | source)
XLA Modules:
  0.0 373.0 jit_solution(2582818840867256101)
XLA Ops:
  15.0 2.9 collective-permute-start
  18.1 2.7 collective-permute-start.2
  21.6 3.5 collective-permute-done.2
  26.6 4.6 %collective-permute-done.5.refs_2_ = f32[2,4,768]{2,1,0:T(4,128)S(1)} collective-permute-done((f32[2,4,768]{2,1,0:T(4,128)S(1)}, f32[2,4,768]{2,1,0:T(4,128)S(1)}, u32[]{:S(2)}, u32[]{:S(2)}) %collective-permute-start.5) | collective-permute-done | bytes 24608 | tf_op jit(solution)/shard_map/ppermute | solution.py:773
  34.4 2.5 collective-permute-start.9
  36.9 8.0 %collective-permute-done.9 = bf16[1,576,128]{2,1,0:T(8,128)(2,1)S(1)} collective-permute-done((bf16[1,576,128]{2,1,0:T(8,128)(2,1)}, bf16[1,576,128]{2,1,0:T(8,128)(2,1)S(1)}, u32[]{:S(2)}, u32[]{:S(2)}) %collective-permute-start.9) | collective-permute-done | bytes 147488 | tf_op jit(solution)/shard_map/ppermute | solution.py:640
  47.6 11.4 %collective-permute-done.7.refs_4_.refs_7_ = bf16[8,256,128]{2,1,0:T(8,128)(2,1)S(1)} collective-permute-done((bf16[8,256,128]{2,1,0:T(8,128)(2,1)S(1)}, bf16[8,256,128]{2,1,0:T(8,128)(2,1)S(1)}, u32[]{:S(2)}, u32[]{:S(2)}) %collective-permute-start.7) | collective-permute-done | bytes 524320 | tf_op jit(solution)/shard_map/ppermute | solution.py:640
  66.9 17.4 %all_to_all.65 = f32[32,4,128]{2,1,0:T(4,128)S(1)} all-to-all(f32[32,4,128]{2,1,0:T(4,128)S(1)} %get-tuple-element.241), channel_id=1, replica_groups=mesh['x'=2,'core'=2,'wide'=8] {'x','core','wide'}, dimensions={0} | all-to-all | bytes 131072 | tf_op jit(solution)/shard_map/all_to_all | solution.py:776
  84.5 2.0 collective-permute-start.12
  86.6 8.3 %collective-permute-done.14 = bf16[1,256,128]{2,1,0:T(8,128)(2,1)S(1)} collective-permute-done((bf16[1,256,128]{2,1,0:T(8,128)(2,1)S(1)}, bf16[1,256,128]{2,1,0:T(8,128)(2,1)S(1)}, u32[]{:S(2)}, u32[]{:S(2)}) %collective-permute-start.14) | collective-permute-done | bytes 65568 | tf_op jit(solution)/shard_map/ppermute | solution.py:640
  95.6 11.3 %collective-permute-done.15 = bf16[2,256,128]{2,1,0:T(8,128)(2,1)S(1)} collective-permute-done((bf16[2,256,128]{2,1,0:T(8,128)(2,1)S(1)}, bf16[2,256,128]{2,1,0:T(8,128)(2,1)S(1)}, u32[]{:S(2)}, u32[]{:S(2)}) %collective-permute-start.15) | collective-permute-done | bytes 131104 | tf_op jit(solution)/shard_map/ppermute | solution.py:640
  108.5 3.0 spatial.2
  111.5 3.5 collective-permute-done.16
  117.1 11.9 %all_to_all.66 = f32[32,4,128]{2,1,0:T(4,128)S(1)} all-to-all(f32[32,4,128]{2,1,0:T(4,128)S(1)} %get-tuple-element.254), channel_id=1, replica_groups=mesh['x'=2,'core'=2,'wide'=8] {'x','core','wide'}, dimensions={0} | all-to-all | bytes 131072 | tf_op jit(solution)/shard_map/all_to_all | solution.py:776
  130.5 10.6 %all_to_all.67.refs_0_ = f32[16,16,128]{2,1,0:T(8,128)S(1)} all-to-all(f32[16,16,128]{2,1,0:T(8,128)S(1)} %get-tuple-element.262), channel_id=1, replica_groups=mesh['x'=2,'core'=2,'wide'=8] {'x','wide'}, dimensions={0} | all-to-all | bytes 262144 | tf_op jit(solution)/shard_map/all_to_all | solution.py:776
  142.0 2.5 collective-permute-done.18.refs_2_
  146.1 9.1 %all_to_all.68 = f32[32,4,128]{2,1,0:T(4,128)S(1)} all-to-all(f32[32,4,128]{2,1,0:T(4,128)S(1)} %get-tuple-element.266), channel_id=1, replica_groups=mesh['x'=2,'core'=2,'wide'=8] {'x','core','wide'}, dimensions={0} | all-to-all | bytes 131072 | tf_op jit(solution)/shard_map/all_to_all | solution.py:776
  155.2 2.6 spatial.3
  159.4 9.2 %all_to_all.69 = f32[32,4,128]{2,1,0:T(4,128)S(1)} all-to-all(f32[32,4,128]{2,1,0:T(4,128)S(1)} %get-tuple-element.271), channel_id=1, replica_groups=mesh['x'=2,'core'=2,'wide'=8] {'x','core','wide'}, dimensions={0} | all-to-all | bytes 131072 | tf_op jit(solution)/shard_map/all_to_all | solution.py:776
  169.3 1.7 expand.3
  171.0 11.8 %all_to_all.70.refs_1_ = f32[16,16,128]{2,1,0:T(8,128)S(1)} all-to-all(f32[16,16,128]{2,1,0:T(8,128)S(1)} %get-tuple-element.273), channel_id=1, replica_groups=mesh['x'=2,'core'=2,'wide'=8] {'x','wide'}, dimensions={0} | all-to-all | bytes 262144 | tf_op jit(solution)/shard_map/all_to_all | solution.py:776
  182.7 1.9 last.1
  184.7 10.5 %all_to_all.71.refs_1_ = f32[16,16,128]{2,1,0:T(8,128)S(1)} all-to-all(f32[16,16,128]{2,1,0:T(8,128)S(1)} %get-tuple-element.282), channel_id=1, replica_groups=mesh['x'=2,'core'=2,'wide'=8] {'x','wide'}, dimensions={0} | all-to-all | bytes 262144 | tf_op jit(solution)/shard_map/all_to_all | solution.py:776
  195.2 1.8 expand_back.2
  201.0 9.4 %all_to_all.72 = f32[32,4,128]{2,1,0:T(4,128)S(1)} all-to-all(f32[32,4,128]{2,1,0:T(4,128)S(1)} %get-tuple-element.292), channel_id=1, replica_groups=mesh['x'=2,'core'=2,'wide'=8] {'x','core','wide'}, dimensions={0} | all-to-all | bytes 131072 | tf_op jit(solution)/shard_map/all_to_all | solution.py:776
  210.5 2.4 spatial_back.2
  212.9 2.1 spatial_grad.2
  217.6 14.6 %all_to_all.73 = f32[32,4,128]{2,1,0:T(4,128)S(1)} all-to-all(f32[32,4,128]{2,1,0:T(4,128)S(1)} %get-tuple-element.303), channel_id=1, replica_groups=mesh['x'=2,'core'=2,'wide'=8] {'x','core','wide'}, dimensions={0} | all-to-all | bytes 131072 | tf_op jit(solution)/shard_map/all_to_all | solution.py:776
  238.1 21.2 %all_to_all.74.refs_1_ = f32[16,16,128]{2,1,0:T(8,128)S(1)} all-to-all(f32[16,16,128]{2,1,0:T(8,128)S(1)} %get-tuple-element.316), channel_id=1, replica_groups=mesh['x'=2,'core'=2,'wide'=8] {'x','wide'}, dimensions={0} | all-to-all | bytes 262144 | tf_op jit(solution)/shard_map/all_to_all | solution.py:776
  266.9 9.5 %all_to_all.75 = f32[32,4,128]{2,1,0:T(4,128)S(1)} all-to-all(f32[32,4,128]{2,1,0:T(4,128)S(1)} %get-tuple-element.332), channel_id=1, replica_groups=mesh['x'=2,'core'=2,'wide'=8] {'x','core','wide'}, dimensions={0} | all-to-all | bytes 131072 | tf_op jit(solution)/shard_map/all_to_all | solution.py:776
  276.7 2.7 spatial_back.3
  279.4 2.1 spatial_grad.3
  285.8 11.9 %collective-permute-done.32.refs_6_ = bf16[1,832,128]{2,1,0:T(8,128)(2,1)S(1)} collective-permute-done((bf16[1,832,128]{2,1,0:T(8,128)(2,1)S(1)}, bf16[1,832,128]{2,1,0:T(8,128)(2,1)S(1)}, u32[]{:S(2)}, u32[]{:S(2)}) %collective-permute-start.32) | collective-permute-done | bytes 213024 | tf_op jit(solution)/shard_map/ppermute | solution.py:681
  298.2 10.3 %all_to_all.76 = f32[32,4,128]{2,1,0:T(4,128)S(1)} all-to-all(f32[32,4,128]{2,1,0:T(4,128)S(1)} %get-tuple-element.358), channel_id=1, replica_groups=mesh['x'=2,'core'=2,'wide'=8] {'x','core','wide'}, dimensions={0} | all-to-all | bytes 131072 | tf_op jit(solution)/shard_map/all_to_all | solution.py:776
  315.9 3.7 collective-permute-done.41.refs_5_.refs_3_
  319.6 1.7 collective-permute-done.42.refs_9_.refs_7_
  321.3 3.7 collective-permute-done.40.refs_2_
  330.7 1.6 lamb.3
  334.5 5.1 %collective-permute-done.46.refs_8_ = bf16[1,512,128]{2,1,0:T(8,128)(2,1)S(1)} collective-permute-done((bf16[1,512,128]{2,1,0:T(8,128)(2,1)S(1)}, bf16[1,512,128]{2,1,0:T(8,128)(2,1)S(1)}, u32[]{:S(2)}, u32[]{:S(2)}) %collective-permute-start.46) | collective-permute-done | bytes 131104 | tf_op jit(solution)/shard_map/ppermute | solution.py:681
  339.7 1.9 collective-permute-done.44.refs_3_
  341.6 1.7 collective-permute-start.47
  347.0 2.4 collective-permute-done.43.refs_2_
  350.1 1.7 collective-permute-done.49.refs_9_
  351.8 1.6 lamb.5
  354.2 2.7 all-to-all-start.12
  356.9 2.2 copy.49
  359.1 2.2 copy.50
  361.3 2.6 all-to-all-done.12.refs_0_
  (232 shorter events, 82.5 us)
Async XLA Ops:
  7.2 101.3 %all-gather.3.cloned.1.call-start = ((), (), s32[]{:S(2)}) async-start(), calls=%async_computation.13 | async-start | bytes 4734976 | tf_op jit(solution)/shard_map/all_gather | solution.py:820
  15.0 17.1 %collective-permute-start = (bf16[448,512]{1,0:T(8,128)(2,1)}, bf16[448,512]{1,0:T(8,128)(2,1)S(1)}, u32[]{:S(2)}, u32[]{:S(2)}) collective-permute-start(bf16[448,512]{1,0:T(8,128)(2,1)} %get-tuple-element.237), channel_id=1, source_target_pairs={{0,16},{16,0},{1,17},{17,1},{2,18},{18,2},{3,19},{19,3},{4,20},{20... | collective-permute-start | bytes 1376264 | tf_op jit(solution)/shard_map/ppermute | solution.py:773
  18.0 8.1 %collective-permute-start.4 = (f32[4,768]{1,0:T(4,128)S(1)}, f32[4,768]{1,0:T(4,128)S(1)}, u32[]{:S(2)}, u32[]{:S(2)}) collective-permute-start(f32[4,768]{1,0:T(4,128)S(1)} %reshape.68), channel_id=1, source_target_pairs={{0,8},{8,0},{1,9},{9,1},{2,10},{10,2},{3,11},{11,3},{4,12},{12,4},... | collective-permute-start | bytes 36872 | tf_op jit(solution)/shard_map/ppermute | solution.py:770
  18.1 7.0 %collective-permute-start.2 = (bf16[1,256,128]{2,1,0:T(8,128)(2,1)}, bf16[1,256,128]{2,1,0:T(8,128)(2,1)S(1)}, u32[]{:S(2)}, u32[]{:S(2)}) collective-permute-start(bf16[1,256,128]{2,1,0:T(8,128)(2,1)} %get-tuple-element.238), channel_id=1, source_target_pairs={{0,4},{1,5},{2,6},{3,7},{4,0},{5,1},{6,2},{7,3},{8,12},{9,13},{10,... | collective-permute-start | bytes 196616 | tf_op jit(solution)/shard_map/ppermute | solution.py:640
  25.1 6.9 %collective-permute-start.3 = (bf16[2,256,128]{2,1,0:T(8,128)(2,1)S(1)}, bf16[2,256,128]{2,1,0:T(8,128)(2,1)S(1)}, u32[]{:S(2)}, u32[]{:S(2)}) collective-permute-start(bf16[2,256,128]{2,1,0:T(8,128)(2,1)S(1)} %constant_dynamic-update-slice_fusion), channel_id=1, source_target_pairs={{0,2},{1,3},{2,0},{3,1},{4,6},{5,7},{6,4},{7,5},{8,10},{9,11},{10,... | collective-permute-start | bytes 393224 | tf_op jit(solution)/shard_map/ppermute | solution.py:640
  26.1 5.1 %collective-permute-start.5 = (f32[2,4,768]{2,1,0:T(4,128)S(1)}, f32[2,4,768]{2,1,0:T(4,128)S(1)}, u32[]{:S(2)}, u32[]{:S(2)}) collective-permute-start(f32[2,4,768]{2,1,0:T(4,128)S(1)} %pad_maximum_fusion.1.refs_1_), channel_id=1, source_target_pairs={{0,16},{16,0},{1,17},{17,1},{2,18},{18,2},{3,19},{19,3},{4,20},{20... | collective-permute-start | bytes 73736 | tf_op jit(solution)/shard_map/ppermute | solution.py:773
  32.7 27.1 %collective-permute-start.1 = (bf16[448,1024]{1,0:T(8,128)(2,1)S(1)}, bf16[448,1024]{1,0:T(8,128)(2,1)S(1)}, u32[]{:S(2)}, u32[]{:S(2)}) collective-permute-start(bf16[448,1024]{1,0:T(8,128)(2,1)S(1)} %join.1.refs_1_.refs_2_), channel_id=1, source_target_pairs={{0,8},{8,0},{1,9},{9,1},{2,10},{10,2},{3,11},{11,3},{4,12},{12,4},... | collective-permute-start | bytes 2752520 | tf_op jit(solution)/shard_map/ppermute | solution.py:770
  32.9 12.0 %collective-permute-start.6 = (bf16[4,256,128]{2,1,0:T(8,128)(2,1)S(1)}, bf16[4,256,128]{2,1,0:T(8,128)(2,1)S(1)}, u32[]{:S(2)}, u32[]{:S(2)}) collective-permute-start(bf16[4,256,128]{2,1,0:T(8,128)(2,1)S(1)} %get-tuple-element.493), channel_id=1, source_target_pairs={{0,1},{1,0},{2,3},{3,2},{4,5},{5,4},{6,7},{7,6},{8,24},{9,25},{10,... | collective-permute-start | bytes 786440 | tf_op jit(solution)/shard_map/ppermute | solution.py:640
  34.4 10.5 %collective-permute-start.9 = (bf16[1,576,128]{2,1,0:T(8,128)(2,1)}, bf16[1,576,128]{2,1,0:T(8,128)(2,1)S(1)}, u32[]{:S(2)}, u32[]{:S(2)}) collective-permute-start(bf16[1,576,128]{2,1,0:T(8,128)(2,1)} %get-tuple-element.248), channel_id=1, source_target_pairs={{0,4},{1,5},{2,6},{3,7},{4,0},{5,1},{6,2},{7,3},{8,12},{9,13},{10,... | collective-permute-start | bytes 442376 | tf_op jit(solution)/shard_map/ppermute | solution.py:640
  45.0 14.0 %collective-permute-start.7 = (bf16[8,256,128]{2,1,0:T(8,128)(2,1)S(1)}, bf16[8,256,128]{2,1,0:T(8,128)(2,1)S(1)}, u32[]{:S(2)}, u32[]{:S(2)}) collective-permute-start(bf16[8,256,128]{2,1,0:T(8,128)(2,1)S(1)} %constant_dynamic-update-slice_fusion.4.refs_3_.refs_6_), channel_id=1, source_target_pairs={{0,16},{1,17},{2,18},{3,19},{4,20},{5,21},{6,22},{7,23},{8,9},{9,8... | collective-permute-start | bytes 1572872 | tf_op jit(solution)/shard_map/ppermute | solution.py:640
  46.9 16.6 %collective-permute-start.10 = (bf16[2,576,128]{2,1,0:T(8,128)(2,1)}, bf16[2,576,128]{2,1,0:T(8,128)(2,1)}, u32[]{:S(2)}, u32[]{:S(2)}) collective-permute-start(bf16[2,576,128]{2,1,0:T(8,128)(2,1)} %constant_dynamic-update-slice_fusion.7), channel_id=1, source_target_pairs={{0,2},{1,3},{2,0},{3,1},{4,6},{5,7},{6,4},{7,5},{8,10},{9,11},{10,... | collective-permute-start | bytes 884744 | tf_op jit(solution)/shard_map/ppermute | solution.py:640
  65.5 18.8 %collective-permute-start.11 = (bf16[4,576,128]{2,1,0:T(8,128)(2,1)S(1)}, bf16[4,576,128]{2,1,0:T(8,128)(2,1)S(1)}, u32[]{:S(2)}, u32[]{:S(2)}) collective-permute-start(bf16[4,576,128]{2,1,0:T(8,128)(2,1)S(1)} %constant_dynamic-update-slice_fusion.9), channel_id=1, source_target_pairs={{0,1},{1,0},{2,3},{3,2},{4,5},{5,4},{6,7},{7,6},{8,24},{9,25},{10,... | collective-permute-start | bytes 1769480 | tf_op jit(solution)/shard_map/ppermute | solution.py:640
  84.5 22.4 %collective-permute-start.12 = (bf16[8,576,128]{2,1,0:T(8,128)(2,1)S(1)}, bf16[8,576,128]{2,1,0:T(8,128)(2,1)}, u32[]{:S(2)}, u32[]{:S(2)}) collective-permute-start(bf16[8,576,128]{2,1,0:T(8,128)(2,1)S(1)} %constant_dynamic-update-slice_fusion.11.refs_6_), channel_id=1, source_target_pairs={{0,16},{1,17},{2,18},{3,19},{4,20},{5,21},{6,22},{7,23},{8,9},{9,8... | collective-permute-start | bytes 3538952 | tf_op jit(solution)/shard_map/ppermute | solution.py:640
  86.5 8.4 %collective-permute-start.14 = (bf16[1,256,128]{2,1,0:T(8,128)(2,1)S(1)}, bf16[1,256,128]{2,1,0:T(8,128)(2,1)S(1)}, u32[]{:S(2)}, u32[]{:S(2)}) collective-permute-start(bf16[1,256,128]{2,1,0:T(8,128)(2,1)S(1)} %bitcast.38), channel_id=1, source_target_pairs={{0,4},{1,5},{2,6},{3,7},{4,0},{5,1},{6,2},{7,3},{8,12},{9,13},{10,... | collective-permute-start | bytes 196616 | tf_op jit(solution)/shard_map/ppermute | solution.py:640
  94.9 12.0 %collective-permute-start.15 = (bf16[2,256,128]{2,1,0:T(8,128)(2,1)S(1)}, bf16[2,256,128]{2,1,0:T(8,128)(2,1)S(1)}, u32[]{:S(2)}, u32[]{:S(2)}) collective-permute-start(bf16[2,256,128]{2,1,0:T(8,128)(2,1)S(1)} %constant_dynamic-update-slice_fusion.13), channel_id=1, source_target_pairs={{0,2},{1,3},{2,0},{3,1},{4,6},{5,7},{6,4},{7,5},{8,10},{9,11},{10,... | collective-permute-start | bytes 393224 | tf_op jit(solution)/shard_map/ppermute | solution.py:640
  95.6 13.0 %collective-permute-start.8 = (bf16[448,256]{1,0:T(8,128)(2,1)}, bf16[448,256]{1,0:T(8,128)(2,1)S(1)}, u32[]{:S(2)}, u32[]{:S(2)}) collective-permute-start(bf16[448,256]{1,0:T(8,128)(2,1)} %copy-done.31), channel_id=1, source_target_pairs={{0,8},{8,0},{1,9},{9,1},{2,10},{10,2},{3,11},{11,3},{4,12},{12,4},... | collective-permute-start | bytes 688136 | tf_op jit(solution)/shard_map/ppermute | solution.py:770
  108.3 6.7 %collective-permute-start.16 = (bf16[4,256,128]{2,1,0:T(8,128)(2,1)}, bf16[4,256,128]{2,1,0:T(8,128)(2,1)}, u32[]{:S(2)}, u32[]{:S(2)}) collective-permute-start(bf16[4,256,128]{2,1,0:T(8,128)(2,1)} %constant_dynamic-update-slice_fusion.15), channel_id=1, source_target_pairs={{0,1},{1,0},{2,3},{3,2},{4,5},{5,4},{6,7},{7,6},{8,24},{9,25},{10,... | collective-permute-start | bytes 786440 | tf_op jit(solution)/shard_map/ppermute | solution.py:640
  116.9 12.1 %collective-permute-start.17 = (bf16[8,256,128]{2,1,0:T(8,128)(2,1)S(1)}, bf16[8,256,128]{2,1,0:T(8,128)(2,1)S(1)}, u32[]{:S(2)}, u32[]{:S(2)}) collective-permute-start(bf16[8,256,128]{2,1,0:T(8,128)(2,1)S(1)} %constant_dynamic-update-slice_fusion.17.refs_6_), channel_id=1, source_target_pairs={{0,16},{1,17},{2,18},{3,19},{4,20},{5,21},{6,22},{7,23},{8,9},{9,8... | collective-permute-start | bytes 1572872 | tf_op jit(solution)/shard_map/ppermute | solution.py:640
  117.0 12.0 %collective-permute-start.13 = (bf16[448,256]{1,0:T(8,128)(2,1)S(1)}, bf16[448,256]{1,0:T(8,128)(2,1)S(1)}, u32[]{:S(2)}, u32[]{:S(2)}) collective-permute-start(bf16[448,256]{1,0:T(8,128)(2,1)S(1)} %get-tuple-element.256), channel_id=1, source_target_pairs={{0,8},{8,0},{1,9},{9,1},{2,10},{10,2},{3,11},{11,3},{4,12},{12,4},... | collective-permute-start | bytes 688136 | tf_op jit(solution)/shard_map/ppermute | solution.py:770
  142.0 2.5 collective-permute-start.18
  145.9 9.3 %collective-permute-start.19 = (bf16[448,256]{1,0:T(8,128)(2,1)S(1)}, bf16[448,256]{1,0:T(8,128)(2,1)S(1)}, u32[]{:S(2)}, u32[]{:S(2)}) collective-permute-start(bf16[448,256]{1,0:T(8,128)(2,1)S(1)} %get-tuple-element.268), channel_id=1, source_target_pairs={{0,8},{8,0},{1,9},{9,1},{2,10},{10,2},{3,11},{11,3},{4,12},{12,4},... | collective-permute-start | bytes 688136 | tf_op jit(solution)/shard_map/ppermute | solution.py:770
  168.6 14.2 %collective-permute-start.21 = (bf16[448,512]{1,0:T(8,128)(2,1)S(1)}, bf16[448,512]{1,0:T(8,128)(2,1)S(1)}, u32[]{:S(2)}, u32[]{:S(2)}) collective-permute-start(bf16[448,512]{1,0:T(8,128)(2,1)S(1)} %copy-done.30), channel_id=1, source_target_pairs={{0,16},{16,0},{1,17},{17,1},{2,18},{18,2},{3,19},{19,3},{4,20},{20... | collective-permute-start | bytes 1376264 | tf_op jit(solution)/shard_map/ppermute | solution.py:773
  198.3 12.1 %collective-permute-start.23 = (bf16[8,256,128]{2,1,0:T(8,128)(2,1)S(1)}, bf16[8,256,128]{2,1,0:T(8,128)(2,1)S(1)}, u32[]{:S(2)}, u32[]{:S(2)}) collective-permute-start(bf16[8,256,128]{2,1,0:T(8,128)(2,1)S(1)} %get-tuple-element.288), channel_id=1, source_target_pairs={{0,16},{1,17},{2,18},{3,19},{4,20},{5,21},{6,22},{7,23},{8,9},{9,8... | collective-permute-start | bytes 1572872 | tf_op jit(solution)/shard_map/ppermute | solution.py:681
  215.0 17.1 %collective-permute-start.25 = (bf16[8,576,128]{2,1,0:T(8,128)(2,1)S(1)}, bf16[8,576,128]{2,1,0:T(8,128)(2,1)S(1)}, u32[]{:S(2)}, u32[]{:S(2)}) collective-permute-start(bf16[8,576,128]{2,1,0:T(8,128)(2,1)S(1)} %get-tuple-element.299), channel_id=1, source_target_pairs={{0,16},{1,17},{2,18},{3,19},{4,20},{5,21},{6,22},{7,23},{8,9},{9,8... | collective-permute-start | bytes 3538952 | tf_op jit(solution)/shard_map/ppermute | solution.py:681
  233.8 2.9 collective-permute-start.26
  234.0 25.4 %collective-permute-start.27 = (bf16[4,832,128]{2,1,0:T(8,128)(2,1)S(1)}, bf16[4,832,128]{2,1,0:T(8,128)(2,1)S(1)}, u32[]{:S(2)}, u32[]{:S(2)}) collective-permute-start(bf16[4,832,128]{2,1,0:T(8,128)(2,1)S(1)} %add_up.10), channel_id=1, source_target_pairs={{0,1},{1,0},{2,3},{3,2},{4,5},{5,4},{6,7},{7,6},{8,24},{9,25},{10,... | collective-permute-start | bytes 2555912 | tf_op jit(solution)/shard_map/ppermute | solution.py:681
  259.5 16.9 %collective-permute-start.30 = (bf16[8,256,128]{2,1,0:T(8,128)(2,1)S(1)}, bf16[8,256,128]{2,1,0:T(8,128)(2,1)S(1)}, u32[]{:S(2)}, u32[]{:S(2)}) collective-permute-start(bf16[8,256,128]{2,1,0:T(8,128)(2,1)S(1)} %get-tuple-element.335), channel_id=1, source_target_pairs={{0,16},{1,17},{2,18},{3,19},{4,20},{5,21},{6,22},{7,23},{8,9},{9,8... | collective-permute-start | bytes 1572872 | tf_op jit(solution)/shard_map/ppermute | solution.py:681
  263.1 13.3 %collective-permute-start.29 = (bf16[8,256,128]{2,1,0:T(8,128)(2,1)S(1)}, bf16[8,256,128]{2,1,0:T(8,128)(2,1)S(1)}, u32[]{:S(2)}, u32[]{:S(2)}) collective-permute-start(bf16[8,256,128]{2,1,0:T(8,128)(2,1)S(1)} %get-tuple-element.328), channel_id=1, source_target_pairs={{0,16},{1,17},{2,18},{3,19},{4,20},{5,21},{6,22},{7,23},{8,9},{9,8... | collective-permute-start | bytes 1572872 | tf_op jit(solution)/shard_map/ppermute | solution.py:681
  264.4 12.0 %collective-permute-start.31 = (bf16[2,832,128]{2,1,0:T(8,128)(2,1)S(1)}, bf16[2,832,128]{2,1,0:T(8,128)(2,1)S(1)}, u32[]{:S(2)}, u32[]{:S(2)}) collective-permute-start(bf16[2,832,128]{2,1,0:T(8,128)(2,1)S(1)} %add_up.11), channel_id=1, source_target_pairs={{0,2},{1,3},{2,0},{3,1},{4,6},{5,7},{6,4},{7,5},{8,10},{9,11},{10,... | collective-permute-start | bytes 1277960 | tf_op jit(solution)/shard_map/ppermute | solution.py:681
  281.5 27.0 %collective-permute-start.36 = (bf16[8,576,128]{2,1,0:T(8,128)(2,1)S(1)}, bf16[8,576,128]{2,1,0:T(8,128)(2,1)S(1)}, u32[]{:S(2)}, u32[]{:S(2)}) collective-permute-start(bf16[8,576,128]{2,1,0:T(8,128)(2,1)S(1)} %get-tuple-element.353), channel_id=1, source_target_pairs={{0,16},{1,17},{2,18},{3,19},{4,20},{5,21},{6,22},{7,23},{8,9},{9,8... | collective-permute-start | bytes 3538952 | tf_op jit(solution)/shard_map/ppermute | solution.py:681
  283.0 14.7 %collective-permute-start.33 = (bf16[4,256,128]{2,1,0:T(8,128)(2,1)S(1)}, bf16[4,256,128]{2,1,0:T(8,128)(2,1)S(1)}, u32[]{:S(2)}, u32[]{:S(2)}) collective-permute-start(bf16[4,256,128]{2,1,0:T(8,128)(2,1)S(1)} %get-tuple-element.344), channel_id=1, source_target_pairs={{0,1},{1,0},{2,3},{3,2},{4,5},{5,4},{6,7},{7,6},{8,24},{9,25},{10,... | collective-permute-start | bytes 786440 | tf_op jit(solution)/shard_map/ppermute | solution.py:681
  283.8 14.1 %collective-permute-start.34 = (bf16[4,256,128]{2,1,0:T(8,128)(2,1)S(1)}, bf16[4,256,128]{2,1,0:T(8,128)(2,1)S(1)}, u32[]{:S(2)}, u32[]{:S(2)}) collective-permute-start(bf16[4,256,128]{2,1,0:T(8,128)(2,1)S(1)} %get-tuple-element.345), channel_id=1, source_target_pairs={{0,1},{1,0},{2,3},{3,2},{4,5},{5,4},{6,7},{7,6},{8,24},{9,25},{10,... | collective-permute-start | bytes 786440 | tf_op jit(solution)/shard_map/ppermute | solution.py:681
  285.1 12.8 %collective-permute-start.35 = (bf16[448,256]{1,0:T(8,128)(2,1)S(1)}, bf16[448,256]{1,0:T(8,128)(2,1)S(1)}, u32[]{:S(2)}, u32[]{:S(2)}) collective-permute-start(bf16[448,256]{1,0:T(8,128)(2,1)S(1)} %get-tuple-element.356), channel_id=1, source_target_pairs={{0,8},{8,0},{1,9},{9,1},{2,10},{10,2},{3,11},{11,3},{4,12},{12,4},... | collective-permute-start | bytes 688136 | tf_op jit(solution)/shard_map/ppermute | solution.py:770
  285.1 12.6 %collective-permute-start.32 = (bf16[1,832,128]{2,1,0:T(8,128)(2,1)S(1)}, bf16[1,832,128]{2,1,0:T(8,128)(2,1)S(1)}, u32[]{:S(2)}, u32[]{:S(2)}) collective-permute-start(bf16[1,832,128]{2,1,0:T(8,128)(2,1)S(1)} %get-tuple-element.346), channel_id=1, source_target_pairs={{0,4},{1,5},{2,6},{3,7},{4,0},{5,1},{6,2},{7,3},{8,12},{9,13},{10,... | collective-permute-start | bytes 638984 | tf_op jit(solution)/shard_map/ppermute | solution.py:681
  310.0 16.8 %collective-permute-start.38 = (bf16[448,1024]{1,0:T(8,128)(2,1)S(1)}, bf16[448,1024]{1,0:T(8,128)(2,1)S(1)}, u32[]{:S(2)}, u32[]{:S(2)}) collective-permute-start(bf16[448,1024]{1,0:T(8,128)(2,1)S(1)} %get-tuple-element.372), channel_id=1, source_target_pairs={{0,8},{8,0},{1,9},{9,1},{2,10},{10,2},{3,11},{11,3},{4,12},{12,4},... | collective-permute-start | bytes 2752520 | tf_op jit(solution)/shard_map/ppermute | solution.py:770
  310.1 14.8 %collective-permute-start.40 = (bf16[4,576,128]{2,1,0:T(8,128)(2,1)S(1)}, bf16[4,576,128]{2,1,0:T(8,128)(2,1)S(1)}, u32[]{:S(2)}, u32[]{:S(2)}) collective-permute-start(bf16[4,576,128]{2,1,0:T(8,128)(2,1)S(1)} %add_up.13), channel_id=1, source_target_pairs={{0,1},{1,0},{2,3},{3,2},{4,5},{5,4},{6,7},{7,6},{8,24},{9,25},{10,... | collective-permute-start | bytes 1769480 | tf_op jit(solution)/shard_map/ppermute | solution.py:681
  312.4 12.7 %collective-permute-start.39 = (bf16[8,256,128]{2,1,0:T(8,128)(2,1)S(1)}, bf16[8,256,128]{2,1,0:T(8,128)(2,1)S(1)}, u32[]{:S(2)}, u32[]{:S(2)}) collective-permute-start(bf16[8,256,128]{2,1,0:T(8,128)(2,1)S(1)} %get-tuple-element.370), channel_id=1, source_target_pairs={{0,16},{1,17},{2,18},{3,19},{4,20},{5,21},{6,22},{7,23},{8,9},{9,8... | collective-permute-start | bytes 1572872 | tf_op jit(solution)/shard_map/ppermute | solution.py:681
  313.1 6.4 %collective-permute-start.41 = (bf16[2,256,128]{2,1,0:T(8,128)(2,1)S(1)}, bf16[2,256,128]{2,1,0:T(8,128)(2,1)S(1)}, u32[]{:S(2)}, u32[]{:S(2)}) collective-permute-start(bf16[2,256,128]{2,1,0:T(8,128)(2,1)S(1)} %get-tuple-element.379), channel_id=1, source_target_pairs={{0,2},{1,3},{2,0},{3,1},{4,6},{5,7},{6,4},{7,5},{8,10},{9,11},{10,... | collective-permute-start | bytes 393224 | tf_op jit(solution)/shard_map/ppermute | solution.py:681
  313.7 7.6 %collective-permute-start.42 = (bf16[2,256,128]{2,1,0:T(8,128)(2,1)S(1)}, bf16[2,256,128]{2,1,0:T(8,128)(2,1)S(1)}, u32[]{:S(2)}, u32[]{:S(2)}) collective-permute-start(bf16[2,256,128]{2,1,0:T(8,128)(2,1)S(1)} %get-tuple-element.380), channel_id=1, source_target_pairs={{0,2},{1,3},{2,0},{3,1},{4,6},{5,7},{6,4},{7,5},{8,10},{9,11},{10,... | collective-permute-start | bytes 393224 | tf_op jit(solution)/shard_map/ppermute | solution.py:681
  325.2 8.3 %collective-permute-start.45 = (bf16[4,256,128]{2,1,0:T(8,128)(2,1)S(1)}, bf16[4,256,128]{2,1,0:T(8,128)(2,1)S(1)}, u32[]{:S(2)}, u32[]{:S(2)}) collective-permute-start(bf16[4,256,128]{2,1,0:T(8,128)(2,1)S(1)} %get-tuple-element.394), channel_id=1, source_target_pairs={{0,1},{1,0},{2,3},{3,2},{4,5},{5,4},{6,7},{7,6},{8,24},{9,25},{10,... | collective-permute-start | bytes 786440 | tf_op jit(solution)/shard_map/ppermute | solution.py:681
  326.1 18.6 %collective-permute-start.37 = (bf16[448,512]{1,0:T(8,128)(2,1)S(1)}, bf16[448,512]{1,0:T(8,128)(2,1)S(1)}, u32[]{:S(2)}, u32[]{:S(2)}) collective-permute-start(bf16[448,512]{1,0:T(8,128)(2,1)S(1)} %get-tuple-element.368), channel_id=1, source_target_pairs={{0,16},{16,0},{1,17},{17,1},{2,18},{18,2},{3,19},{19,3},{4,20},{20... | collective-permute-start | bytes 1376264 | tf_op jit(solution)/shard_map/ppermute | solution.py:773
  327.6 21.8 %collective-permute-start.43 = (bf16[448,512]{1,0:T(8,128)(2,1)S(1)}, bf16[448,512]{1,0:T(8,128)(2,1)S(1)}, u32[]{:S(2)}, u32[]{:S(2)}) collective-permute-start(bf16[448,512]{1,0:T(8,128)(2,1)S(1)} %get-tuple-element.399), channel_id=1, source_target_pairs={{0,16},{16,0},{1,17},{17,1},{2,18},{18,2},{3,19},{19,3},{4,20},{20... | collective-permute-start | bytes 1376264 | tf_op jit(solution)/shard_map/ppermute | solution.py:773
  329.1 12.4 %collective-permute-start.44 = (bf16[2,576,128]{2,1,0:T(8,128)(2,1)S(1)}, bf16[2,576,128]{2,1,0:T(8,128)(2,1)S(1)}, u32[]{:S(2)}, u32[]{:S(2)}) collective-permute-start(bf16[2,576,128]{2,1,0:T(8,128)(2,1)S(1)} %add_up.15), channel_id=1, source_target_pairs={{0,2},{1,3},{2,0},{3,1},{4,6},{5,7},{6,4},{7,5},{8,10},{9,11},{10,... | collective-permute-start | bytes 884744 | tf_op jit(solution)/shard_map/ppermute | solution.py:681
  329.8 9.8 %collective-permute-start.46 = (bf16[1,512,128]{2,1,0:T(8,128)(2,1)S(1)}, bf16[1,512,128]{2,1,0:T(8,128)(2,1)S(1)}, u32[]{:S(2)}, u32[]{:S(2)}) collective-permute-start(bf16[1,512,128]{2,1,0:T(8,128)(2,1)S(1)} %get-tuple-element.400), channel_id=1, source_target_pairs={{0,4},{1,5},{2,6},{3,7},{4,0},{5,1},{6,2},{7,3},{8,12},{9,13},{10,... | collective-permute-start | bytes 393224 | tf_op jit(solution)/shard_map/ppermute | solution.py:681
  333.6 10.1 %collective-permute-start.48 = (bf16[2,256,128]{2,1,0:T(8,128)(2,1)S(1)}, bf16[2,256,128]{2,1,0:T(8,128)(2,1)S(1)}, u32[]{:S(2)}, u32[]{:S(2)}) collective-permute-start(bf16[2,256,128]{2,1,0:T(8,128)(2,1)S(1)} %add_up.17), channel_id=1, source_target_pairs={{0,2},{1,3},{2,0},{3,1},{4,6},{5,7},{6,4},{7,5},{8,10},{9,11},{10,... | collective-permute-start | bytes 393224 | tf_op jit(solution)/shard_map/ppermute | solution.py:681
  341.6 10.2 %collective-permute-start.47 = (bf16[1,576,128]{2,1,0:T(8,128)(2,1)S(1)}, bf16[1,576,128]{2,1,0:T(8,128)(2,1)S(1)}, u32[]{:S(2)}, u32[]{:S(2)}) collective-permute-start(bf16[1,576,128]{2,1,0:T(8,128)(2,1)S(1)} %add_up.18), channel_id=1, source_target_pairs={{0,4},{1,5},{2,6},{3,7},{4,0},{5,1},{6,2},{7,3},{8,12},{9,13},{10,... | collective-permute-start | bytes 442376 | tf_op jit(solution)/shard_map/ppermute | solution.py:681
  343.7 8.1 %collective-permute-start.49 = (bf16[1,256,128]{2,1,0:T(8,128)(2,1)S(1)}, bf16[1,256,128]{2,1,0:T(8,128)(2,1)S(1)}, u32[]{:S(2)}, u32[]{:S(2)}) collective-permute-start(bf16[1,256,128]{2,1,0:T(8,128)(2,1)S(1)} %add_up.19), channel_id=1, source_target_pairs={{0,4},{1,5},{2,6},{3,7},{4,0},{5,1},{6,2},{7,3},{8,12},{9,13},{10,... | collective-permute-start | bytes 196616 | tf_op jit(solution)/shard_map/ppermute | solution.py:681
  354.2 9.7 %all-to-all-start.12 = ((f32[32,1,128]{2,1,0:T(1,128)}), f32[32,1,128]{2,1,0:T(1,128)S(1)}, u32[]{:S(2)}, u32[]{:S(2)}) async-start(f32[32,1,128]{2,1,0:T(1,128)} %get-tuple-element.449), calls=%async_computation.12 | async-start | bytes 32768 | tf_op jit(solution)/shard_map/all_to_all | solution.py:776
  (40 other events, 234.3 us)
Sparse Core Ops, SparseCore 0:
  12.3 95.9 all-gather.2
